TPU v7x, 512 devices: a whole 4x4x16 slice. The times are simulated.
512 devices in a mesh: uly: 4 (over z_lo), row: 8 (over x, core), col: 16 (over z_hi, y).
Axes of the slice: x: 4, y: 4, z: 16 (z_hi: 4, z_lo: 4; z = z_hi * 4 + z_lo), core: 2. Of those that a mesh axis runs over, the one named last changes fastest.
Arguments:
- queries: bfloat16 [1024, 4096], P(('row', 'col', 'uly')), may hold values from -8 to 8
- keys: bfloat16 [65536, 1024], P(('col', 'row', 'uly')), may hold values from -8 to 8
- values: bfloat16 [65536, 1024], P(('col', 'row', 'uly')), may hold values from -6 to 6
- window_blocks: int32 [16], replicated, may hold values from 0 to 1023, as said below
Outputs:
- attended: bfloat16 [1024, 4096], P(('row', 'col', 'uly'))
Inputs may be any that keep to these rules, and one draw needn't show every extreme that they name: `window_blocks`: distinct blocks of 64 positions; entries 2r and 2r + 1 are the (r + 1)-th earliest and the (r + 1)-th latest of the 16 blocks; the first and the last block of the sequence are always among them.
All inputs are finite; a program needn't handle non-finite values.
Results may differ from a plain program's by a relative error of at most 0.015.
Values may be sent and summed in bfloat16 or wider, within the bound.
A program may use at most 64 MiB of HBM per device.

v0:
```python
import math

import jax
import jax.numpy as jnp
from jax import lax
from jax.sharding import PartitionSpec as P

QUERY_HEAD_COUNT = 32
KEY_VALUE_HEADS = 8
HEAD_SIZE = 128


def combined_all(value, axis, join):
    pieces = jax.tree.map(lambda part: lax.all_gather(part, axis), value)
    head = jax.tree.map(lambda part: part[0], pieces)
    tail = jax.tree.map(lambda part: part[1:], pieces)
    so_far, _ = lax.scan(lambda so_far, slab: (join(so_far, slab), None), head, tail)
    return so_far


def combine(first_part, second_part):
    max_a, sum_a, acc_a = first_part
    max_b, sum_b, acc_b = second_part
    joined = jnp.maximum(max_a, max_b)
    weight_a = jnp.exp(max_a - joined)
    weight_b = jnp.exp(max_b - joined)
    return (
        joined,
        sum_a * weight_a + sum_b * weight_b,
        acc_a * weight_a[..., None] + acc_b * weight_b[..., None],
    )


def per_device(queries, keys, values, window_blocks):
    n_row = lax.axis_size("row")
    n_col = lax.axis_size("col")
    row_at = lax.axis_index("row")
    col_at = lax.axis_index("col")
    q_heads = lax.all_to_all(queries, "uly", split_axis=1, concat_axis=0, tiled=True)
    k_heads, v_heads = (
        lax.all_to_all(keys, "uly", split_axis=1, concat_axis=0, tiled=True),
        lax.all_to_all(values, "uly", split_axis=1, concat_axis=0, tiled=True),
    )
    piece_len = k_heads.shape[0]
    width_kv = k_heads.shape[1]
    kv_local = width_kv // HEAD_SIZE
    queries_per_group = QUERY_HEAD_COUNT // KEY_VALUE_HEADS
    q_rows = lax.all_gather(q_heads, "col", axis=0, tiled=True)
    row_count = q_rows.shape[0]
    block_rows = row_count // 2
    score_scale = 1.0 / math.sqrt(HEAD_SIZE)
    starts = lax.dynamic_slice_in_dim(window_blocks, 2 * row_at, 2)
    within = jnp.arange(block_rows, dtype=jnp.int32)
    query_pos = starts[:, None] * block_rows + within[None, :]
    query_block_tiles = q_rows.reshape(2, block_rows, kv_local, queries_per_group, HEAD_SIZE)
    col_span = n_row * piece_len

    def positions(start, piece_rows):
        return col_at * col_span + start + jnp.arange(piece_rows, dtype=jnp.int32)

    def tile_step(carry_in, k_block, v_block, k_pos):
        block_len = k_block.shape[0]
        k_tile = k_block.reshape(block_len, kv_local, HEAD_SIZE)
        v_tile = v_block.reshape(block_len, kv_local, HEAD_SIZE)
        lowest = jnp.min(k_pos)
        max_all, sum_all, acc_all = carry_in
        updated = []
        for half_index in range(2):

            def update(kept, half_index=half_index):
                row_max, row_sum, row_acc = kept
                scores = (
                    jnp.einsum(
                        "qhgd,khd->hgqk",
                        query_block_tiles[half_index],
                        k_tile,
                        preferred_element_type=jnp.float32,
                    )
                    * score_scale
                )
                visible = k_pos[None, :] <= query_pos[half_index][:, None]
                scores = jnp.where(visible, scores, -1e30)
                new_max = jnp.maximum(row_max, jnp.max(scores, axis=-1))
                weights = jnp.where(visible, jnp.exp(scores - new_max[..., None]), 0.0)
                rescale = jnp.exp(row_max - new_max)
                new_sum = row_sum * rescale + jnp.sum(weights, axis=-1)
                new_acc = row_acc * rescale[..., None] + jnp.einsum(
                    "hgqk,khd->hgqd",
                    weights.astype(jnp.bfloat16),
                    v_tile,
                    preferred_element_type=jnp.float32,
                )
                return (new_max, new_sum, new_acc)

            updated.append(
                lax.cond(
                    lowest <= query_pos[half_index, -1],
                    update,
                    lambda kept: kept,
                    (max_all[half_index], sum_all[half_index], acc_all[half_index]),
                )
            )
        return (
            jnp.stack([item[0] for item in updated]),
            jnp.stack([item[1] for item in updated]),
            jnp.stack([item[2] for item in updated]),
        )

    init_max = jnp.full((2, kv_local, queries_per_group, block_rows), -1e30, jnp.float32)
    init_sum = jnp.zeros((2, kv_local, queries_per_group, block_rows), jnp.float32)
    init_acc = jnp.zeros((2, kv_local, queries_per_group, block_rows, HEAD_SIZE), jnp.float32)
    k_piece = lax.all_gather(k_heads, "row", axis=0, tiled=True)
    v_piece = lax.all_gather(v_heads, "row", axis=0, tiled=True)
    piece_rows = k_piece.shape[0]
    block_len = 128

    def block_step(block_index, carry_now):
        k_block = lax.dynamic_slice_in_dim(k_piece, block_index * block_len, block_len, 0)
        v_block = lax.dynamic_slice_in_dim(v_piece, block_index * block_len, block_len, 0)
        return tile_step(carry_now, k_block, v_block, positions(block_index * block_len, block_len))

    max_all, sum_all, acc_all = lax.fori_loop(
        0, piece_rows // block_len, block_step, (init_max, init_sum, init_acc)
    )
    max_rows = max_all.transpose(1, 2, 0, 3).reshape(kv_local, queries_per_group, row_count)
    sum_rows = sum_all.transpose(1, 2, 0, 3).reshape(kv_local, queries_per_group, row_count)
    acc_rows = acc_all.transpose(1, 2, 0, 3, 4).reshape(
        kv_local, queries_per_group, row_count, HEAD_SIZE
    )
    share_rows = row_count // n_col
    max_total, sum_total, acc_total = combined_all((max_rows, sum_rows, acc_rows), "col", combine)
    acc_own = lax.dynamic_slice_in_dim(acc_total, col_at * share_rows, share_rows, 2)
    sum_own = lax.dynamic_slice_in_dim(sum_total, col_at * share_rows, share_rows, 2)
    result = (acc_own / sum_own[..., None]).transpose(2, 0, 1, 3)
    result = result.reshape(share_rows, kv_local * queries_per_group * HEAD_SIZE).astype(
        jnp.bfloat16
    )
    return lax.all_to_all(result, "uly", split_axis=0, concat_axis=1, tiled=True)


def solution(mesh):
    return jax.shard_map(
        per_device,
        mesh=mesh,
        in_specs=(
            P(("row", "col", "uly"), None),
            P(("col", "row", "uly"), None),
            P(("col", "row", "uly"), None),
            P(),
        ),
        out_specs=P(("row", "col", "uly"), None),
        check_vma=False,
    )
```

profile of v0, /device:TPU:1, one launch (start us, length us, event | category | flops | bytes accessed | tf_op | source)
XLA Modules:
  0.0 834.7 jit_solution(12705309074625262968)
XLA Ops:
  7.7 12.2 %all_to_all.73 = bf16[128,4,256]{0,2,1:T(8,128)(2,1)S(1)} all-to-all(bf16[128,4,256]{0,2,1:T(8,128)(2,1)S(1)} %bitcast.144), channel_id=1, replica_groups=mesh['uly'=4,'row'=8,'col'=16] {'uly'}, dimensions={1} | all-to-all | bytes 524288 | tf_op jit(solution)/shard_map/all_to_all | solution.py:41
  21.9 8.6 %all_to_all.74 = bf16[128,4,256]{0,2,1:T(8,128)(2,1)S(1)} all-to-all(bf16[128,4,256]{0,2,1:T(8,128)(2,1)S(1)} %bitcast.145), channel_id=1, replica_groups=mesh['uly'=4,'row'=8,'col'=16] {'uly'}, dimensions={1} | all-to-all | bytes 524288 | tf_op jit(solution)/shard_map/all_to_all | solution.py:42
  39.1 55.9 %all_gather.20 = bf16[128,1024]{1,0:T(8,128)(2,1)S(1)} all-gather(bf16[8,1024]{1,0:T(8,128)(2,1)S(1)} %all_to_all.65), channel_id=1, replica_groups=mesh['uly'=4,'row'=8,'col'=16] {'col'}, dimensions={0}, use_global_device_ids=true | all-gather | bytes 278528 | tf_op jit(solution)/shard_map/all_gather | solution.py:48
  95.4 456.0 %while.33 = (s32[]{:T(128)}, f32[2,2,4,64]{3,2,1,0:T(4,128)S(1)}, f32[2,2,4,64]{3,2,1,0:T(4,128)S(1)}, f32[2,2,4,64,128]{4,3,2,1,0:T(8,128)S(1)}, s32[]{:T(128)}...) while((s32[]{:T(128)}, f32[2,2,4,64]{3,2,1,0:T(4,128)S(1)}, ...), condition=%wide.region_10.11_spmd, body=%wide.region_0.10_spmd.sunk | while | flops 68702472 | bytes 5934543 | solution.py:122
  115.2 3.6 conditional.5
  130.0 3.6 conditional.5
  144.8 3.6 conditional.5
  159.6 3.6 conditional.5
  174.4 3.6 conditional.5
  189.3 3.6 conditional.5
  204.1 3.6 conditional.5
  218.9 3.6 conditional.5
  233.7 3.6 conditional.5
  248.5 3.6 conditional.5
  263.3 3.6 conditional.5
  278.1 3.6 conditional.5
  292.9 3.6 conditional.5
  307.8 3.6 conditional.5
  322.6 3.6 conditional.5
  337.4 3.6 conditional.5
  352.2 3.6 conditional.5
  367.0 3.6 conditional.5
  381.8 3.6 conditional.5
  396.6 3.6 conditional.5
  411.4 3.6 conditional.5
  441.1 3.6 conditional.5
  552.4 38.5 %all_gather.21 = f32[16,2,4,128]{3,2,1,0:T(4,128)S(1)} all-gather(f32[1,2,4,128]{3,2,1,0:T(4,128)S(1)} %all_gather_reshape.9), channel_id=1, replica_groups=mesh['uly'=4,'row'=8,'col'=16] {'col'}, dimensions={0}, use_global_device_ids=true | all-gather | bytes 69632 | tf_op jit(solution)/shard_map/all_gather | solution.py:14
  591.0 51.4 %all_gather.22 = f32[16,2,4,128]{3,2,1,0:T(4,128)S(1)} all-gather(f32[1,2,4,128]{3,2,1,0:T(4,128)S(1)} %all_gather_reshape.10), channel_id=1, replica_groups=mesh['uly'=4,'row'=8,'col'=16] {'col'}, dimensions={0}, use_global_device_ids=true | all-gather | bytes 69632 | tf_op jit(solution)/shard_map/all_gather | solution.py:14
  642.4 144.6 %all-gather.8.cloned.1.call-done = f32[16,2,4,128,128]{4,3,2,1,0:T(8,128)} async-done(((f32[1,2,4,128,128]{4,3,2,1,0:T(8,128)}), f32[16,2,4,128,128]{4,3,2,1,0:T(8,128)}) %all-gather.8.cloned.1.call-update) | async-done | bytes 8388624 | tf_op jit(solution)/shard_map/all_gather | solution.py:14
  787.0 7.3 slice.113
  795.4 23.5 %while.34 = (s32[]{:T(128)}, f32[2,4,128]{2,1,0:T(4,128)S(1)}, f32[2,4,128]{2,1,0:T(4,128)S(1)}, f32[2,4,128,128]{3,2,1,0:T(8,128)S(1)}, f32[15,2,4,128]{3,2,1,0...) while((s32[]{:T(128)}, f32[2,4,128]{2,1,0:T(4,128)S(1)}, ...), condition=%wide.region_12.13_spmd, body=%wide.region_11.12_spmd.sunk | while | flops 399362 | bytes 1613917 | solution.py:17
  819.1 8.4 %all_to_all.75 = bf16[4,2,1024]{2,1,0:T(2,128)(2,1)S(1)} all-to-all(bf16[4,2,1024]{2,1,0:T(2,128)(2,1)S(1)} %convert_element_type.36), channel_id=1, replica_groups=mesh['uly'=4,'row'=8,'col'=16] {'uly'}, dimensions={0} | all-to-all | bytes 32768 | tf_op jit(solution)/shard_map/all_to_all | solution.py:138
  (906 shorter events, 542.1 us)
Async XLA Ops:
  6.5 88.7 %all-gather.4.cloned.1.call-start = ((), (), s32[]{:S(2)}) async-start(), calls=%async_computation.4 | async-start | bytes 2359296 | tf_op jit(solution)/shard_map/all_gather | solution.py:112
  20.8 74.5 %all-gather.6.cloned.1.call-start = ((), (), s32[]{:S(2)}) async-start(), calls=%async_computation.5 | async-start | bytes 2359296 | tf_op jit(solution)/shard_map/all_gather | solution.py:113
  31.4 7.7 all-to-all-start.2
  34.7 752.3 %all-gather.8.cloned.1.call-start = ((), (), s32[]{:S(2)}) async-start(), calls=%async_computation.6 | async-start | bytes 8912896 | tf_op jit(solution)/shard_map/all_gather | solution.py:14
Sparse Core Ops, SparseCore 0:
  20.9 38.1 all-gather.3
  61.2 33.1 all-gather.5
  552.4 234.5 all-gather.7
where the time goes:
time: 848 us; the launch traced here: 835 us
  other arithmetic  204 us (24%)
  blocking collectives  175 us (21%)
  waiting for transfers between devices  148 us (17%)
  local copies, waits for them, and re-layouts  135 us (16%)
  loops' own time  83.3 us (10%)
  matrix products  72.4 us (9%)
  between operations  13.3 us (2%)
    all_gather x1, waiting for transfers between devices, combined_all(): pieces = jax.tree.map(lambda part: lax.all_gather(part, axis), value)  145 us
    all_gather x2, blocking collectives, combined_all(): pieces = jax.tree.map(lambda part: lax.all_gather(part, axis), value)  89.9 us
    another operation x1, loops' own time, per_device(): lax.fori_loop(0, piece_rows // block_len, block_step, (init_max, init_sum...  81.1 us
    all_gather x1, blocking collectives, per_device(): q_rows = lax.all_gather(q_heads, 'col', axis=0, tiled=True)  55.9 us
    reduce_sum x59, other arithmetic, update(): new_sum = row_sum * rescale + jnp.sum(weights, axis=-1)  55.8 us
    dot_general x59, matrix products, update(): jnp.einsum('hgqk,khd->hgqd', weights.astype(jnp.bfloat16), v_tile, prefer...  55.2 us
    while x64, local copies, waits for them, and re-layouts  43.3 us
    another operation x91, other arithmetic, tile_step(): jnp.stack([item[1] for item in updated])  40.9 us
  transfers between devices with their start and end apart: 4, of which 2 were waited for; matrix products, arithmetic and copies ran while one was open for 0% of the time, Pallas kernels for 0%

commit v1 on v0

v1 whole, which is shorter than its diff:
```python
import math

import jax
import jax.numpy as jnp
from jax import lax
from jax.experimental import pallas as pl
from jax.experimental.pallas import tpu as pltpu
from jax.sharding import PartitionSpec as P

HEAD = 128
MESH = pl.DeviceIdType.MESH
SCALE = math.log2(math.e) / math.sqrt(HEAD)
HIDDEN = -1e30
F32, BF16 = jnp.float32, jnp.bfloat16


def expand(row):
    return jnp.transpose(jnp.broadcast_to(row, (HEAD, HEAD)))


def kernel(
    q_ref, k_ref, v_ref, wb_ref, out_ref,
    q_out, q_in, q_all, k_all, v_all, thr,
    o_all, l_all, o_in, l_in,
    p_out, lp_out, p_in, lp_in,
    z_out, lz_out, z_in, lz_in, f_out, f_in,
    q1s, q1r, ks, kr, vs, vr, own_sem,
    q2s, q2r, q3s, q3r, q4s, q4r,
    osn, orc, lsn, lrc, psn, prc, lpsn, lprc,
    zsn, zrc, lzsn, lzrc, fsn, frc,
):
    u = lax.axis_index("uly")
    row = lax.axis_index("row")
    col = lax.axis_index("col")
    x, core = row // 2, row % 2
    y = col % 4
    z = (col // 4) * 4 + u

    def dev(x_at, y_at, z_at, core_at):
        z_at = (z_at + 16) % 16
        return {
            "uly": z_at % 4,
            "row": (x_at % 4) * 2 + core_at,
            "col": (z_at // 4) * 4 + y_at % 4,
        }

    def remote(src, dst, send, recv, to):
        return pltpu.make_async_remote_copy(
            src_ref=src, dst_ref=dst, send_sem=send, recv_sem=recv,
            device_id=to, device_id_type=MESH,
        )

    d2 = 2 - 4 * core
    targets = [(z, 1 - core, 1)]
    targets += [(z + 1, c, 2 + core) for c in range(2)]
    targets += [(z - 1, c, 4 + core) for c in range(2)]
    targets += [(z + d2, c, 6 + core) for c in range(2)]
    sources = [(z, 1 - core), (z - 1, 0), (z - 1, 1), (z + 1, 0), (z + 1, 1), (z - 2, 0), (z + 2, 1)]
    peers = [dev(x, y, zt, c) for zt, c, _ in targets] + [dev(x, y, z - d2, core)]
    peers += [dev(x, y, z + 4 * i, core) for i in range(1, 4)]
    peers += [dev(x + i, y, z, core) for i in range(1, 4)]
    peers += [dev(x, y + i, z, core) for i in range(1, 4)]

    def group_of(zt, c):
        return 2 * ((zt + 16) % 4) + c

    my_group = group_of(z, core)

    v_all[:, :, HEAD:] = jnp.ones((8, HEAD, HEAD), BF16)
    l_all[...] = jnp.zeros_like(l_all)
    lp_out[...] = jnp.zeros_like(lp_out)
    lz_out[...] = jnp.zeros_like(lz_out)
    barrier = pltpu.get_barrier_semaphore()
    for peer in peers:
        pl.semaphore_signal(barrier, inc=1, device_id=peer, device_id_type=MESH)
    for h in range(32):
        q_out[h // 4, 2 * (h % 4):2 * (h % 4) + 2, :] = q_ref[:, h * HEAD:(h + 1) * HEAD].astype(F32)
    pl.semaphore_wait(barrier, len(peers))

    sends = []

    def go(copy):
        copy.start()
        sends.append(copy)

    for n, (zt, c, slot) in enumerate(targets):
        go(remote(q_out.at[group_of(zt, c)], q_in.at[slot], q1s.at[n], q1r.at[slot], dev(x, y, zt, c)))

    def features(ref, group):
        return ref.at[:, pl.ds(pl.multiple_of(group * HEAD, HEAD), HEAD)]

    for n, (zt, c, slot) in enumerate(targets):
        to, group = dev(x, y, zt, c), group_of(zt, c)
        go(remote(features(k_ref, group), k_all.at[slot], ks.at[n], kr.at[slot], to))
        go(remote(features(v_ref, group), v_all.at[slot, :, pl.ds(0, HEAD)], vs.at[n], vr.at[slot], to))
    own_k = pltpu.make_async_copy(features(k_ref, my_group), k_all.at[0], own_sem.at[0])
    own_v = pltpu.make_async_copy(features(v_ref, my_group), v_all.at[0, :, pl.ds(0, HEAD)], own_sem.at[1])
    own_k.start()
    own_v.start()

    me = dev(x, y, z, 1 - core)

    def arrived(ref, sem):
        remote(ref, ref, sem, sem, me).wait_recv()

    q_in[0] = q_out[my_group]
    for slot in range(1, 8):
        arrived(q_in.at[slot], q1r.at[slot])
    q_all[0, 0, 0:64, :] = q_in[...].reshape(64, HEAD).astype(BF16)

    def z_place(ref, r):
        return ref.at[r // 2, 0, pl.ds((r % 2) * 64, 64)]

    for i in range(1, 4):
        go(remote(z_place(q_all, 0), z_place(q_all, 4 - i), q2s.at[i], q2r.at[4 - i], dev(x, y, z + 4 * i, core)))

    blk = lax.broadcasted_iota(jnp.int32, (32, HEAD), 0)
    lane = lax.broadcasted_iota(jnp.int32, (32, HEAD), 1)
    half, step, sub = (blk >> 2) & 1, blk >> 3, blk & 3
    ys = (y + jnp.where(half == 0, step, sub)) & 3
    xs = (x + jnp.where(half == 0, sub, step)) & 3
    slot = (lane >> 3) & 7
    cs = jnp.where(slot == 0, core, jnp.where(slot == 1, 1 - core, slot & 1))
    dz = jnp.where(slot < 2, 0, jnp.where(slot < 4, -1, jnp.where(slot < 6, 1, jnp.where(slot == 6, -2, 2))))
    zs = (z + 4 * (2 * half + (lane >> 6)) + dz + 16) & 15
    which = 2 * (2 * xs + cs) + (zs >> 3)
    block_at = jnp.zeros((32, HEAD), jnp.int32)
    for i in range(16):
        block_at = jnp.where(which == i, wb_ref[i], block_at)
    pos = 64 * block_at + ((((zs >> 2) & 1) * 4 + ys) * 8 + (zs & 3) * 2 + (lane & 1))
    pos = pos.astype(F32)
    for b in range(32):
        thr[b] = expand(pos[b:b + 1, :])

    arrived(z_place(q_all, 1), q2r.at[1])
    for i in range(1, 4):
        go(remote(q_all.at[0, 0], q_all.at[0, 4 - i], q3s.at[0, i], q3r.at[0, 4 - i], dev(x + i, y, z, core)))
    arrived(z_place(q_all, 2), q2r.at[2])
    arrived(z_place(q_all, 3), q2r.at[3])
    for i in range(1, 4):
        go(remote(q_all.at[1, 0], q_all.at[1, 4 - i], q3s.at[1, i], q3r.at[1, 4 - i], dev(x, y + i, z, core)))
    for r in range(1, 4):
        arrived(q_all.at[0, r], q3r.at[0, r])
    for i in range(1, 4):
        go(remote(q_all.at[0], q_all.at[2 * (4 - i)], q4s.at[2 * i], q4r.at[2 * (4 - i)], dev(x, y + i, z, core)))
    for r in range(1, 4):
        arrived(q_all.at[1, r], q3r.at[1, r])
    for i in range(1, 4):
        go(remote(q_all.at[1], q_all.at[2 * (4 - i) + 1], q4s.at[2 * i + 1], q4r.at[2 * (4 - i) + 1], dev(x + i, y, z, core)))

    own_k.wait()
    own_v.wait()
    for slot in range(1, 8):
        arrived(k_all.at[slot], kr.at[slot])
        arrived(v_all.at[slot, :, pl.ds(0, HEAD)], vr.at[slot])

    lane_f = lax.broadcasted_iota(jnp.int32, (1, HEAD), 1).astype(F32)
    key_pos = []
    for zt, c in [(z, core)] + sources:
        zt = (zt + 16) % 16
        base = (zt // 4) * 16384 + y * 4096 + x * 1024 + c * 512 + (zt % 4) * 128
        key_pos.append(lane_f + base.astype(F32))
    eye = lax.broadcasted_iota(jnp.int32, (HEAD, HEAD), 0) == lax.broadcasted_iota(jnp.int32, (HEAD, HEAD), 1)

    def squeeze(wide):
        return jnp.sum(jnp.where(eye, wide, 0.0), axis=0, keepdims=True)

    def result_copies(k):
        t, half = k // 2, k % 2
        to = dev(x + t * half, y + t * (1 - half), z, core)
        there = 2 * (4 - t) + half
        return (
            remote(o_all.at[k], o_in.at[there], osn.at[k], orc.at[there], to),
            remote(l_all.at[k], l_in.at[there], lsn.at[k], lrc.at[there], to),
        )

    def chunk(k, carry):
        @pl.when(k >= 2)
        def _():
            arrived(q_all.at[k], q4r.at[k])

        for pair in range(2):
            q = q_all[k, 2 * pair:2 * pair + 2].reshape(256, HEAD)
            scores = lax.dot_general(
                q, k_all[...].reshape(1024, HEAD), (((1,), (1,)), ((), ())), preferred_element_type=F32
            )
            limit = thr[pl.ds(4 * k + 2 * pair, 2)].reshape(256, HEAD)
            parts = [
                jnp.where(key_pos[j] <= limit, scores[:, j * HEAD:(j + 1) * HEAD], HIDDEN) for j in range(8)
            ]
            top = parts[0]
            for part in parts[1:]:
                top = jnp.maximum(top, part)
            top = jnp.max(top, axis=1, keepdims=True) * SCALE
            weights = jnp.concatenate([jnp.exp2(part * SCALE - top).astype(BF16) for part in parts], axis=1)
            both = lax.dot_general(
                weights, v_all[...].reshape(1024, 2 * HEAD), (((1,), (0,)), ((), ())), preferred_element_type=F32
            )
            total = both[:, HEAD:]
            o_all[k, pl.ds(256 * pair, 256), :] = (both[:, :HEAD] / total).astype(BF16)
            level = top + jnp.log2(total)
            for b in range(2):
                l_all[k, 2 * pair + b:2 * pair + b + 1, :] = squeeze(level[b * HEAD:(b + 1) * HEAD])

        @pl.when(k >= 2)
        def _():
            for copy in result_copies(k):
                copy.start()

        return carry

    lax.fori_loop(0, 8, chunk, 0)

    def combine(levels, values):
        top = levels[0]
        for level in levels[1:]:
            top = jnp.maximum(top, level)
        shares = [jnp.exp2(level - top) for level in levels]
        total = shares[0] + shares[1] + shares[2] + shares[3]
        inverse = 1.0 / total
        return top + jnp.log2(total), [share * inverse for share in shares]

    def weighted(shares, values):
        acc = expand(shares[0]) * values[0].astype(F32)
        for share, value in zip(shares[1:], values[1:]):
            acc = acc + expand(share) * value.astype(F32)
        return acc

    for half in range(2):
        for t in range(1, 4):
            arrived(o_in.at[2 * t + half], orc.at[2 * t + half])
            arrived(l_in.at[2 * t + half], lrc.at[2 * t + half])
        for b in (1, 2, 3, 0):
            levels = [l_all[half, b:b + 1, :]] + [l_in[2 * t + half, b:b + 1, :] for t in range(1, 4)]
            level, shares = combine(levels, None)
            rows = slice(b * HEAD, (b + 1) * HEAD)
            values = [o_all[half, rows, :]] + [o_in[2 * t + half, rows, :] for t in range(1, 4)]
            p_out[half, b] = weighted(shares, values).astype(BF16)
            lp_out[half, b, 0:1, :] = level
            if b:
                to = dev(x + b * (1 - half), y + b * half, z, core)
                go(remote(p_out.at[half, b], p_in.at[half, 4 - b], psn.at[half, b], prc.at[half, 4 - b], to))
                go(remote(lp_out.at[half, b], lp_in.at[half, 4 - b], lpsn.at[half, b], lprc.at[half, 4 - b], to))

    for half in range(2):
        for b in range(1, 4):
            arrived(p_in.at[half, b], prc.at[half, b])
            arrived(lp_in.at[half, b], lprc.at[half, b])
        levels = [lp_out[half, 0, 0:1, :]] + [lp_in[half, b, 0:1, :] for b in range(1, 4)]
        level, shares = combine(levels, None)
        values = [p_out[half, 0]] + [p_in[half, b] for b in range(1, 4)]
        z_out[half] = weighted(shares, values).astype(BF16)
        lz_out[half, 0:1, :] = level
        for i in (2 * half, 2 * half + 1):
            if i:
                to = dev(x, y, z + 4 * i, core)
                go(remote(z_out.at[half, pl.ds((i % 2) * 64, 64)], z_in.at[4 - i], zsn.at[i], zrc.at[4 - i], to))
                go(remote(lz_out.at[half], lz_in.at[4 - i], lzsn.at[i], lzrc.at[4 - i], to))

    for i in range(1, 4):
        arrived(z_in.at[i], zrc.at[i])
        arrived(lz_in.at[i], lzrc.at[i])
    levels = [expand(lz_out[0, 0:1, :])[:64]]
    levels += [expand(lz_in[i, 0:1, :])[(i % 2) * 64:(i % 2) * 64 + 64] for i in range(1, 4)]
    _, shares = combine(levels, None)
    result = shares[0] * z_out[0, 0:64, :].astype(F32)
    for i in range(1, 4):
        result = result + shares[i] * z_in[i].astype(F32)
    f_out[...] = result.reshape(8, 8, HEAD)
    for slot, (zt, c) in enumerate(sources, 1):
        go(remote(f_out.at[slot], f_in.at[my_group], fsn.at[slot], frc.at[my_group], dev(x, y, zt, c)))
    f_in[my_group] = f_out[0]
    for zt, c, _ in targets:
        group = group_of(zt, c)
        arrived(f_in.at[group], frc.at[group])
    for h in range(32):
        out_ref[:, h * HEAD:(h + 1) * HEAD] = f_in[h // 4, 2 * (h % 4):2 * (h % 4) + 2, :].astype(BF16)

    for copy in sends:
        copy.wait_send()
    for k in range(2, 8):
        for copy in result_copies(k):
            copy.wait_send()


def per_device(queries, keys, values, window_blocks):
    dma = pltpu.SemaphoreType.DMA
    vmem = pltpu.VMEM
    return pl.pallas_call(
        kernel,
        out_shape=jax.ShapeDtypeStruct(queries.shape, BF16),
        in_specs=[
            pl.BlockSpec(memory_space=pltpu.VMEM),
            pl.BlockSpec(memory_space=pl.ANY),
            pl.BlockSpec(memory_space=pl.ANY),
            pl.BlockSpec(memory_space=pltpu.SMEM),
        ],
        out_specs=pl.BlockSpec(memory_space=pltpu.VMEM),
        scratch_shapes=[
            vmem((8, 8, HEAD), F32), vmem((8, 8, HEAD), F32),
            vmem((8, 4, HEAD, HEAD), BF16), vmem((8, HEAD, HEAD), BF16), vmem((8, HEAD, 2 * HEAD), BF16),
            vmem((32, HEAD, HEAD), F32),
            vmem((8, 512, HEAD), BF16), vmem((8, 8, HEAD), F32), vmem((8, 512, HEAD), BF16), vmem((8, 8, HEAD), F32),
            vmem((2, 4, HEAD, HEAD), BF16), vmem((2, 4, 8, HEAD), F32),
            vmem((2, 4, HEAD, HEAD), BF16), vmem((2, 4, 8, HEAD), F32),
            vmem((2, HEAD, HEAD), BF16), vmem((2, 8, HEAD), F32),
            vmem((4, 64, HEAD), BF16), vmem((4, 8, HEAD), F32),
            vmem((8, 8, HEAD), F32), vmem((8, 8, HEAD), F32),
            dma((7,)), dma((8,)), dma((7,)), dma((8,)), dma((7,)), dma((8,)), dma((2,)),
            dma((4,)), dma((4,)), dma((2, 4)), dma((2, 4)), dma((8,)), dma((8,)),
            dma((8,)), dma((8,)), dma((8,)), dma((8,)),
            dma((2, 4)), dma((2, 4)), dma((2, 4)), dma((2, 4)),
            dma((4,)), dma((4,)), dma((4,)), dma((4,)), dma((8,)), dma((8,)),
        ],
        compiler_params=pltpu.CompilerParams(
            collective_id=0, has_side_effects=True, vmem_limit_bytes=40 * 1024 * 1024
        ),
    )(queries, keys, values, window_blocks)


def solution(mesh):
    return jax.shard_map(
        per_device,
        mesh=mesh,
        in_specs=(
            P(("row", "col", "uly"), None),
            P(("col", "row", "uly"), None),
            P(("col", "row", "uly"), None),
            P(),
        ),
        out_specs=P(("row", "col", "uly"), None),
        check_vma=False,
    )
```

time: 848 us -> 73.9 us (0.09); the launches traced: 835 us -> 73.7 us
  other arithmetic: 204 us -> 0 us
  blocking collectives: 175 us -> 0 us
  waiting for transfers between devices: 148 us -> 0 us
  local copies, waits for them, and re-layouts: 135 us -> 3.88 us
  loops' own time: 83.3 us -> 0 us
  matrix products: 72.4 us -> 0 us
  Pallas kernels: 0 us -> 69.8 us
  between operations: 13.3 us -> 0.01 us
    all_gather x3 -> x0, blocking collectives: 146 us -> none  [the longest x2 89.9 us: combined_all(): pieces = jax.tree.map(lambda part: lax.all_gather(part, axis), value)]
    all_gather x3 -> x0, waiting for transfers between devices: 145 us -> none  [the longest x1 145 us: combined_all(): pieces = jax.tree.map(lambda part: lax.all_gather(part, axis), value)]
    another operation x66 -> x0, loops' own time: 83.3 us -> none  [the longest x1 81.1 us: per_device(): lax.fori_loop(0, piece_rows // block_len, block_step, (init_max, init_sum...]
    dot_general x118 -> x0, matrix products: 72.4 us -> none  [the longest x59 55.2 us: update(): jnp.einsum('hgqk,khd->hgqd', weights.astype(jnp.bfloat16), v_tile, prefer...]
    pallas_call x0 -> x1, Pallas kernels: none -> 69.8 us  [per_device(): pl.pallas_call(kernel, out_shape=jax.ShapeDtypeStruct(queries.shape, BF16...]
    another operation x155 -> x0, other arithmetic: 64.4 us -> none  [the longest x91 40.9 us: tile_step(): jnp.stack([item[1] for item in updated])]
    reduce_sum x59 -> x0, other arithmetic: 55.8 us -> none  [update(): new_sum = row_sum * rescale + jnp.sum(weights, axis=-1)]
    add x63 -> x0, other arithmetic: 43.8 us -> none  [the longest x15 22.8 us: combine(): acc_a * weight_a[..., None] + acc_b * weight_b[..., None]]
  transfers between devices with their start and end apart: 4 -> 0, of which waited for: 2 -> 0; matrix products, arithmetic and copies ran while one was open for 0% -> 0% of each run, Pallas kernels for 0% -> 0%
where the time goes in v1:
time: 73.9 us; the launch traced here: 73.7 us
  Pallas kernels  69.8 us (94%)
  local copies, waits for them, and re-layouts  3.88 us (5%)
    pallas_call x1, Pallas kernels, per_device(): pl.pallas_call(kernel, out_shape=jax.ShapeDtypeStruct(queries.shape, BF16...  69.8 us
    unnamed x9, local copies, waits for them, and re-layouts  3.88 us

profile of v1, /device:TPU:1, one launch (start us, length us, event | category | flops | bytes accessed | tf_op | source)
XLA Modules:
  0.0 73.7 jit_solution(13559777012265319539)
XLA Ops:
  0.0 0.0 copy-start
  0.0 0.9 %copy-done = bf16[128,1024]{1,0:T(8,128)(2,1)S(1)} copy-done((bf16[128,1024]{1,0:T(8,128)(2,1)S(1)}, bf16[128,1024]{1,0:T(8,128)(2,1)}, u32[]{:S(2)}) %copy-start) | copy-done | bytes 262168
  1.0 0.0 copy-start.1
  1.0 0.9 %copy-done.1 = bf16[128,1024]{1,0:T(8,128)(2,1)S(1)} copy-done((bf16[128,1024]{1,0:T(8,128)(2,1)S(1)}, bf16[128,1024]{1,0:T(8,128)(2,1)}, u32[]{:S(2)}) %copy-start.1) | copy-done | bytes 262168
  1.9 0.0 copy-start.2
  1.9 0.7 copy-done.2
  2.6 0.0 copy-start.3
  2.6 0.7 copy-done.3
  3.3 69.8 %shard_map.46 = bf16[2,4096]{1,0:T(2,128)(2,1)S(1)} custom-call(bf16[2,4096]{1,0:T(2,128)(2,1)S(1)} %copy-done.2, bf16[128,1024]{1,0:T(8,128)(2,1)S(1)} %copy-done, bf16[128,1024]{1,0:T(8,128)(2,1)S(1)} %copy-done.1, s32[16]{0:T(128)S(1)} %copy-done.3), custom_call_target="tpu_custom_call" | custom-call | tf_op jit(solution)/shard_map/pallas_call | solution.py:289
  73.0 0.6 copy.6
Async XLA Ops:
  0.0 0.9 %copy-start = (bf16[128,1024]{1,0:T(8,128)(2,1)S(1)}, bf16[128,1024]{1,0:T(8,128)(2,1)}, u32[]{:S(2)}) copy-start(bf16[128,1024]{1,0:T(8,128)(2,1)} %k_ref.1) | copy-start | bytes 786436
  1.0 0.9 %copy-start.1 = (bf16[128,1024]{1,0:T(8,128)(2,1)S(1)}, bf16[128,1024]{1,0:T(8,128)(2,1)}, u32[]{:S(2)}) copy-start(bf16[128,1024]{1,0:T(8,128)(2,1)} %v_ref.1) | copy-start | bytes 786436
  1.9 0.7 copy-start.2
  2.6 0.7 copy-start.3

commit v2 on v0

v2 whole, which is shorter than its diff:
```python
import math

import jax
import jax.numpy as jnp
from jax import lax
from jax.experimental import pallas as pl
from jax.experimental.pallas import tpu as pltpu
from jax.sharding import PartitionSpec as P

HEAD = 128
MESH = pl.DeviceIdType.MESH
SCALE = math.log2(math.e) / math.sqrt(HEAD)
HIDDEN = -1e30
F32, BF16 = jnp.float32, jnp.bfloat16
BLOCK = 128


def expand(row):
    return jnp.transpose(jnp.broadcast_to(row, (HEAD, HEAD)))


def combine(levels):
    top = jnp.maximum(jnp.maximum(levels[0], levels[1]), jnp.maximum(levels[2], levels[3]))
    shares = [jnp.exp2(level - top) for level in levels]
    total = (shares[0] + shares[1]) + (shares[2] + shares[3])
    inverse = 1.0 / total
    return top + jnp.log2(total), [share * inverse for share in shares]


def weighted(shares, values):
    acc = shares[0] * values[0].astype(F32)
    for share, value in zip(shares[1:], values[1:]):
        acc = acc + share * value.astype(F32)
    return acc


def kernel(
    q_ref, k_ref, v_ref, wb_ref, out_ref,
    wb, q_own, q_f32, q_cls, q_z, q_all, k_all, v_all, pos, thr, key_pos,
    o_all, l_all, o_in, l_in, p_out, lp_out, p_in, lp_in,
    z_out, lz_out, z_in, lz_in, s_out, s_in, f_in,
    own, swap, s1, s2, s3, q4s, q4r, kv, osn, orc, lsn, lrc, ps, lps, zs, lzs, fs,
):
    u = lax.axis_index("uly")
    row = lax.axis_index("row")
    col = lax.axis_index("col")
    x, core = row // 2, row % 2
    y = col % 4
    z = (col // 4) * 4 + u

    def dev(x_at, y_at, z_at, core_at):
        z_at = (z_at + 16) % 16
        return {
            "uly": z_at % 4,
            "row": (x_at % 4) * 2 + core_at,
            "col": (z_at // 4) * 4 + y_at % 4,
        }

    def remote(src, dst, sems, to):
        return pltpu.make_async_remote_copy(
            src_ref=src, dst_ref=dst, send_sem=sems[0], recv_sem=sems[1], device_id=to, device_id_type=MESH
        )

    other = dev(x, y, z, 1 - core)

    def pair(sem):
        return sem.at[0], sem.at[1]

    def arrived(ref, sems):
        remote(ref, ref, sems, other).wait_recv()

    def sent(ref, sems):
        remote(ref, ref, sems, other).wait_send()

    def loop(start, stop, body):
        def step(i, carry):
            body(i)
            return carry

        lax.fori_loop(start, stop, step, 0)

    d2 = 2 - 4 * core
    barrier = pltpu.get_barrier_semaphore()

    def greet(to):
        pl.semaphore_signal(barrier, inc=1, device_id=to, device_id_type=MESH)

    def greet_z(j):
        greet(dev(x, y, z + 5 - j, core))
        greet(dev(x, y, z - 5 + j, core))

    def greet_xy(i):
        greet(dev(x + i, y, z, core))
        greet(dev(x, y + i, z, core))

    loop(1, 5, greet_z)
    loop(1, 4, greet_xy)
    greet(dev(x, y, z + 1, 1 - core))
    greet(dev(x, y, z - 1, 1 - core))
    greet(dev(x, y, z + d2, 1 - core))
    greet(other)
    own_q = pltpu.make_async_copy(q_ref, q_own.at[0], own.at[0])
    own_q.start()
    own_wb = pltpu.make_async_copy(wb_ref, wb, own.at[1])
    own_wb.start()

    def features(ref, group):
        return ref.at[:, pl.ds(pl.multiple_of(group * HEAD, HEAD), HEAD)]

    def v_place(slot):
        return v_all.at[slot, :, pl.ds(0, HEAD)]

    my_group = 2 * u + core
    own_k = pltpu.make_async_copy(features(k_ref, my_group), k_all.at[0], own.at[2])
    own_v = pltpu.make_async_copy(features(v_ref, my_group), v_place(0), own.at[3])
    own_k.start()
    own_v.start()
    v_all[:, :, HEAD:] = jnp.ones((8, HEAD, HEAD), BF16)
    own_q.wait()
    own_wb.wait()
    pl.semaphore_wait(barrier, 18)

    remote(q_ref, q_own.at[1], pair(swap), other).start()
    arrived(q_own.at[1], pair(swap))

    def pack(c):
        for r in range(2):
            for g in range(4):
                at = pl.multiple_of(((2 * c + core) * 4 + g) * HEAD, HEAD)
                q_f32[c, 8 * r + 2 * g:8 * r + 2 * g + 2, :] = q_own[r, :, pl.ds(at, HEAD)].astype(F32)
        q_cls[c] = q_f32[c].astype(BF16)

    loop(0, 4, pack)

    def z_rows(at, n):
        return q_z.at[pl.ds(pl.multiple_of(16 * at, 16), 16 * n)]

    def along_z(j):
        d = 5 - j
        remote(q_cls.at[(u + d) % 4], z_rows(4 - d, 1), pair(s1), dev(x, y, z + d, core)).start()
        remote(q_cls.at[(u - d + 4) % 4], z_rows(4 + d, 1), pair(s1), dev(x, y, z - d, core)).start()

    loop(1, 5, along_z)
    q_z[64:80, :] = q_cls[u]

    def spread(group, slot, to):
        remote(features(k_ref, group), k_all.at[slot], (kv.at[0], kv.at[1]), to).start()
        remote(features(v_ref, group), v_place(slot), (kv.at[2], kv.at[3]), to).start()

    def spread_z(c):
        for d, slot in ((1, 2 + core), (-1, 4 + core), (d2, 6 + core)):
            spread(2 * ((u + d + 4) % 4) + c, slot, dev(x, y, z + d, c))

    loop(0, 2, spread_z)
    spread(2 * u + 1 - core, 1, other)

    blk = lax.broadcasted_iota(jnp.int32, (32, HEAD), 0)
    lane = lax.broadcasted_iota(jnp.int32, (32, HEAD), 1)
    half, step, sub = blk >> 4, (blk >> 2) & 3, blk & 3
    ys = (y + jnp.where(half == 0, step, sub)) & 3
    xs = (x + jnp.where(half == 0, sub, step)) & 3
    cs = jnp.where((lane & 8) == 0, core, 1 - core)
    z_src = (z + 8 * half + (lane >> 4) + 12) & 15
    which = 2 * (2 * xs + cs) + (z_src >> 3)
    block_at = jnp.zeros((32, HEAD), jnp.int32)
    for i in range(16):
        block_at = jnp.where(which == i, wb[i], block_at)
    within = (((z_src >> 2) & 1) * 4 + ys) * 8 + (z_src & 3) * 2 + (lane & 1)
    pos[...] = (64 * block_at + within).astype(F32)
    lane_f = lax.broadcasted_iota(jnp.int32, (1, HEAD), 1).astype(F32)
    sources = [(z, core), (z, 1 - core), (z - 1, 0), (z - 1, 1), (z + 1, 0), (z + 1, 1), (z - 2, 0), (z + 2, 1)]
    for j, (zt, c) in enumerate(sources):
        zt = (zt + 16) % 16
        base = (zt // 4) * 16384 + y * 4096 + x * 1024 + c * 512 + (zt % 4) * 128
        key_pos[j:j + 1, :] = lane_f + base.astype(F32)

    def spread_pos(b):
        thr[b] = expand(pos[pl.ds(b, 1), :])

    def first_peer(h, i):
        return dev(x + i * (1 - h), y + i * h, z, core)

    def second_peer(h, i):
        return dev(x + i * h, y + i * (1 - h), z, core)

    def first(h):
        def go(i):
            remote(q_z.at[pl.ds(128 * h, 128)], q_all.at[h, 0, 4 - i], (s3.at[h, 0], s3.at[h, 1]), first_peer(h, i)).start()

        loop(1, 4, go)
        q_all[h, 0, 0] = q_z[128 * h:128 * h + 128, :]

    def second(h):
        arrived(q_all.at[h, 0, pl.ds(1, 3)], (s3.at[h, 0], s3.at[h, 1]))

        def go(i):
            remote(q_all.at[h, 0], q_all.at[h, 4 - i], (q4s.at[h], q4r.at[h, 4 - i]), second_peer(h, i)).start()

        loop(1, 4, go)

    arrived(q_z.at[pl.ds(0, 128)], pair(s1))
    remote(z_rows(5, 4), z_rows(9, 4), pair(s2), dev(x, y, z - 4, core)).start()
    remote(z_rows(1, 3), z_rows(13, 3), pair(s2), dev(x, y, z + 4, core)).start()
    first(0)
    loop(0, 32, spread_pos)
    second(0)
    arrived(z_rows(9, 7), pair(s2))
    first(1)

    own_k.wait()
    own_v.wait()
    arrived(k_all.at[pl.ds(1, 7)], (kv.at[0], kv.at[1]))
    arrived(v_all.at[pl.ds(1, 7), :, pl.ds(0, HEAD)], (kv.at[2], kv.at[3]))

    eye = lax.broadcasted_iota(jnp.int32, (HEAD, HEAD), 0) == lax.broadcasted_iota(jnp.int32, (HEAD, HEAD), 1)

    def chunk(i):
        code = i - ((i + 6) // 8 - (i + 3) // 8) + 3 * ((i + 7) // 8 - (i + 6) // 8)
        h, t = code // 4, code % 4

        @pl.when(i == 1)
        def _():
            second(1)

        @pl.when(i >= 2)
        def _():
            arrived(q_all.at[h, t], (q4s.at[h], q4r.at[h, t]))

        def block(b):
            q = q_all[h, t, b]
            scores = lax.dot_general(
                q, k_all[...].reshape(1024, HEAD), (((1,), (1,)), ((), ())), preferred_element_type=F32
            )
            limit = thr[code * 4 + b]
            parts = [
                jnp.where(key_pos[j:j + 1, :] <= limit, scores[:, j * HEAD:(j + 1) * HEAD], HIDDEN) for j in range(8)
            ]
            top = parts[0]
            for part in parts[1:]:
                top = jnp.maximum(top, part)
            top = jnp.max(top, axis=1, keepdims=True) * SCALE
            weights = jnp.concatenate([jnp.exp2(part * SCALE - top).astype(BF16) for part in parts], axis=1)
            both = lax.dot_general(
                weights, v_all[...].reshape(1024, 2 * HEAD), (((1,), (0,)), ((), ())), preferred_element_type=F32
            )
            total = both[:, HEAD:]
            o_all[h, t, b] = (both[:, :HEAD] / total).astype(BF16)
            level = top + jnp.log2(total)
            l_all[h, t, pl.ds(b, 1), :] = jnp.sum(jnp.where(eye, level, 0.0), axis=0, keepdims=True)

        loop(0, 4, block)

        @pl.when(i >= 2)
        def _():
            to = second_peer(h, t)
            remote(o_all.at[h, t], o_in.at[h, 4 - t], (osn.at[h], orc.at[h]), to).start()
            remote(l_all.at[h, t], l_in.at[h, 4 - t], (lsn.at[h], lrc.at[h]), to).start()

    loop(0, 8, chunk)

    def join_second(h):
        arrived(o_in.at[h, pl.ds(1, 3)], (osn.at[h], orc.at[h]))
        arrived(l_in.at[h, pl.ds(1, 3)], (lsn.at[h], lrc.at[h]))

        def block(i):
            b = (i + 1) % 4
            level, shares = combine([l_all[h, 0, pl.ds(b, 1), :]] + [l_in[h, t, pl.ds(b, 1), :] for t in range(1, 4)])
            values = [o_all[h, 0, b]] + [o_in[h, t, b] for t in range(1, 4)]
            p_out[h, b] = weighted([expand(share) for share in shares], values).astype(BF16)
            lp_out[h, b] = level

            @pl.when(i < 3)
            def _():
                to = first_peer(h, b)
                remote(p_out.at[h, b], p_in.at[h, 4 - b], (ps.at[h, 0], ps.at[h, 1]), to).start()
                remote(lp_out.at[h, b], lp_in.at[h, 4 - b], (lps.at[h, 0], lps.at[h, 1]), to).start()

        loop(0, 4, block)

    loop(0, 2, join_second)

    def z_part(ref, s):
        return ref.at[pl.ds(pl.multiple_of(16 * s, 16), 16)]

    def join_first(h):
        arrived(p_in.at[h, pl.ds(1, 3)], (ps.at[h, 0], ps.at[h, 1]))
        arrived(lp_in.at[h, pl.ds(1, 3)], (lps.at[h, 0], lps.at[h, 1]))
        level, shares = combine([lp_out[h, 0]] + [lp_in[h, b] for b in range(1, 4)])
        values = [p_out[h, 0]] + [p_in[h, b] for b in range(1, 4)]
        joined = weighted([expand(share) for share in shares], values).astype(BF16)
        z_out[pl.ds(pl.multiple_of(128 * h, 128), 128), :] = joined
        lz_out[h] = level

        def go(i):
            s = 8 * h + i

            @pl.when(s != 4)
            def _():
                to = dev(x, y, z + s - 4, core)
                at = (20 - s) % 16
                remote(z_part(z_out, s), z_in.at[at], pair(zs), to).start()
                remote(lz_out.at[h], lz_in.at[at], pair(lzs), to).start()

        loop(0, 8, go)

    loop(0, 2, join_first)
    z_in[0] = z_out[64:80, :]
    lz_in[0] = lz_out[0]
    arrived(z_in.at[pl.ds(1, 15)], pair(zs))
    arrived(lz_in.at[pl.ds(1, 15)], pair(lzs))
    lane16 = lax.broadcasted_iota(jnp.int32, (16, HEAD), 1) - lax.broadcasted_iota(jnp.int32, (16, HEAD), 0)

    def join_z(w):
        levels, values = [], []
        for m in range(4):
            at = w + 4 * m
            offset = ((20 - at) % 8) * 16
            wide = jnp.broadcast_to(lz_in[at], (16, HEAD))
            levels.append(jnp.sum(jnp.where(lane16 == offset, wide, 0.0), axis=1, keepdims=True))
            values.append(z_in[at])
        _, shares = combine(levels)
        joined = weighted(shares, values)
        f_in[2 * ((u + w) % 4) + core] = joined[:8]
        s_out[w] = joined[8:]

    loop(0, 4, join_z)
    remote(s_out, s_in, pair(fs), other).start()
    arrived(s_in, pair(fs))

    def place(w):
        f_in[2 * ((u + w) % 4) + 1 - core] = s_in[w]

    loop(0, 4, place)

    def give(c):
        for g in range(4):
            at = pl.multiple_of((4 * c + g) * HEAD, HEAD)
            out_ref[:, pl.ds(at, HEAD)] = f_in[c, 2 * g:2 * g + 2, :].astype(BF16)

    loop(0, 8, give)

    sent(q_own.at[1], pair(swap))
    sent(q_z.at[pl.ds(0, 128)], pair(s1))
    sent(z_rows(9, 7), pair(s2))
    sent(k_all.at[pl.ds(1, 7)], (kv.at[0], kv.at[1]))
    sent(v_all.at[pl.ds(1, 7), :, pl.ds(0, HEAD)], (kv.at[2], kv.at[3]))
    for h in range(2):
        sent(q_all.at[h, 0, pl.ds(1, 3)], (s3.at[h, 0], s3.at[h, 1]))
        sent(q_all.at[h, pl.ds(1, 3)], (q4s.at[h], q4r.at[h, 0]))
        sent(o_in.at[h, pl.ds(1, 3)], (osn.at[h], orc.at[h]))
        sent(l_in.at[h, pl.ds(1, 3)], (lsn.at[h], lrc.at[h]))
        sent(p_in.at[h, pl.ds(1, 3)], (ps.at[h, 0], ps.at[h, 1]))
        sent(lp_in.at[h, pl.ds(1, 3)], (lps.at[h, 0], lps.at[h, 1]))
    sent(z_in.at[pl.ds(1, 15)], pair(zs))
    sent(lz_in.at[pl.ds(1, 15)], pair(lzs))
    sent(s_in, pair(fs))


def per_device(queries, keys, values, window_blocks):
    dma = pltpu.SemaphoreType.DMA
    vmem = pltpu.VMEM
    return pl.pallas_call(
        kernel,
        out_shape=jax.ShapeDtypeStruct(queries.shape, BF16),
        in_specs=[pl.BlockSpec(memory_space=pl.ANY)] * 4,
        out_specs=pl.BlockSpec(memory_space=pltpu.VMEM),
        scratch_shapes=[
            pltpu.SMEM((16,), jnp.int32),
            vmem((2, 2, 4096), BF16), vmem((4, 16, HEAD), F32), vmem((4, 16, HEAD), BF16), vmem((256, HEAD), BF16),
            vmem((2, 4, 4, HEAD, HEAD), BF16), vmem((8, HEAD, HEAD), BF16), vmem((8, HEAD, 2 * HEAD), BF16),
            vmem((32, HEAD), F32), vmem((32, HEAD, HEAD), F32), vmem((8, HEAD), F32),
            vmem((2, 4, 4, HEAD, HEAD), BF16), vmem((2, 4, 4, HEAD), F32),
            vmem((2, 4, 4, HEAD, HEAD), BF16), vmem((2, 4, 4, HEAD), F32),
            vmem((2, 4, HEAD, HEAD), BF16), vmem((2, 4, 1, HEAD), F32),
            vmem((2, 4, HEAD, HEAD), BF16), vmem((2, 4, 1, HEAD), F32),
            vmem((256, HEAD), BF16), vmem((2, 1, HEAD), F32),
            vmem((16, 16, HEAD), BF16), vmem((16, 1, HEAD), F32),
            vmem((4, 8, HEAD), F32), vmem((4, 8, HEAD), F32), vmem((8, 8, HEAD), F32),
            dma((4,)), dma((2,)), dma((2,)), dma((2,)), dma((2, 2)), dma((2,)), dma((2, 4)), dma((4,)),
            dma((2,)), dma((2,)), dma((2,)), dma((2,)), dma((2, 2)), dma((2, 2)), dma((2,)), dma((2,)), dma((2,)),
        ],
        compiler_params=pltpu.CompilerParams(
            collective_id=0, has_side_effects=True, vmem_limit_bytes=58 * 1024 * 1024
        ),
    )(queries, keys, values, window_blocks)


def solution(mesh):
    return jax.shard_map(
        per_device,
        mesh=mesh,
        in_specs=(
            P(("row", "col", "uly"), None),
            P(("col", "row", "uly"), None),
            P(("col", "row", "uly"), None),
            P(),
        ),
        out_specs=P(("row", "col", "uly"), None),
        check_vma=False,
    )
```

time: 848 us -> 71.2 us (0.08); the launches traced: 835 us -> 71 us
  other arithmetic: 204 us -> 0 us
  blocking collectives: 175 us -> 0 us
  waiting for transfers between devices: 148 us -> 0 us
  local copies, waits for them, and re-layouts: 135 us -> 1.34 us
  loops' own time: 83.3 us -> 0 us
  matrix products: 72.4 us -> 0 us
  Pallas kernels: 0 us -> 69.6 us
  between operations: 13.3 us -> 0.01 us
    all_gather x3 -> x0, blocking collectives: 146 us -> none  [the longest x2 89.9 us: combined_all(): pieces = jax.tree.map(lambda part: lax.all_gather(part, axis), value)]
    all_gather x3 -> x0, waiting for transfers between devices: 145 us -> none  [the longest x1 145 us: combined_all(): pieces = jax.tree.map(lambda part: lax.all_gather(part, axis), value)]
    another operation x66 -> x0, loops' own time: 83.3 us -> none  [the longest x1 81.1 us: per_device(): lax.fori_loop(0, piece_rows // block_len, block_step, (init_max, init_sum...]
    dot_general x118 -> x0, matrix products: 72.4 us -> none  [the longest x59 55.2 us: update(): jnp.einsum('hgqk,khd->hgqd', weights.astype(jnp.bfloat16), v_tile, prefer...]
    pallas_call x0 -> x1, Pallas kernels: none -> 69.6 us  [per_device(): pl.pallas_call(kernel, out_shape=jax.ShapeDtypeStruct(queries.shape, BF16...]
    another operation x155 -> x0, other arithmetic: 64.4 us -> none  [the longest x91 40.9 us: tile_step(): jnp.stack([item[1] for item in updated])]
    reduce_sum x59 -> x0, other arithmetic: 55.8 us -> none  [update(): new_sum = row_sum * rescale + jnp.sum(weights, axis=-1)]
    add x63 -> x0, other arithmetic: 43.8 us -> none  [the longest x15 22.8 us: combine(): acc_a * weight_a[..., None] + acc_b * weight_b[..., None]]
  transfers between devices with their start and end apart: 4 -> 0, of which waited for: 2 -> 0; matrix products, arithmetic and copies ran while one was open for 0% -> 0% of each run, Pallas kernels for 0% -> 0%
where the time goes in v2:
time: 71.2 us; the launch traced here: 71 us
  Pallas kernels  69.6 us (98%)
  local copies, waits for them, and re-layouts  1.34 us (2%)
    pallas_call x1, Pallas kernels, per_device(): pl.pallas_call(kernel, out_shape=jax.ShapeDtypeStruct(queries.shape, BF16...  69.6 us

profile of v2, /device:TPU:1, one launch (start us, length us, event | category | flops | bytes accessed | tf_op | source)
XLA Modules:
  0.0 71.0 jit_solution(5755391056914356265)
XLA Ops:
  0.0 69.6 %shard_map.46 = bf16[2,4096]{1,0:T(2,128)(2,1)} custom-call(bf16[2,4096]{1,0:T(2,128)(2,1)} %q_ref.1, bf16[128,1024]{1,0:T(8,128)(2,1)} %k_ref.1, bf16[128,1024]{1,0:T(8,128)(2,1)} %v_ref.1, s32[16]{0:T(128)} %wb_ref.1), custom_call_target="tpu_custom_call" | custom-call | tf_op jit(solution)/shard_map/pallas_call | solution.py:362
  69.6 1.3 %copy.6 = bf16[2,4096]{1,0:T(2,128)(2,1)} copy(bf16[2,4096]{1,0:T(2,128)(2,1)} %shard_map.46) | data formatting | bytes 32768

commit v3 on v2

--- a/solution.py
+++ b/solution.py
@@ -12,7 +12,6 @@
 SCALE = math.log2(math.e) / math.sqrt(HEAD)
 HIDDEN = -1e30
 F32, BF16 = jnp.float32, jnp.bfloat16
-BLOCK = 128
 
 
 def expand(row):
@@ -142,17 +141,6 @@
 
     loop(1, 5, along_z)
     q_z[64:80, :] = q_cls[u]
-
-    def spread(group, slot, to):
-        remote(features(k_ref, group), k_all.at[slot], (kv.at[0], kv.at[1]), to).start()
-        remote(features(v_ref, group), v_place(slot), (kv.at[2], kv.at[3]), to).start()
-
-    def spread_z(c):
-        for d, slot in ((1, 2 + core), (-1, 4 + core), (d2, 6 + core)):
-            spread(2 * ((u + d + 4) % 4) + c, slot, dev(x, y, z + d, c))
-
-    loop(0, 2, spread_z)
-    spread(2 * u + 1 - core, 1, other)
 
     blk = lax.broadcasted_iota(jnp.int32, (32, HEAD), 0)
     lane = lax.broadcasted_iota(jnp.int32, (32, HEAD), 1)
@@ -184,28 +172,51 @@
         return dev(x + i * h, y + i * (1 - h), z, core)
 
     def first(h):
+        mine = q_z.at[pl.ds(128 * h, 128)]
+
         def go(i):
-            remote(q_z.at[pl.ds(128 * h, 128)], q_all.at[h, 0, 4 - i], (s3.at[h, 0], s3.at[h, 1]), first_peer(h, i)).start()
+            remote(mine, q_all.at[h, 0, 4 - i], (s3.at[h, 0], s3.at[h, 4 - i]), first_peer(h, i)).start()
+
+        def go_on(i):
+            remote(mine, q_all.at[h, 4 - i, 0], (q4s.at[h], q4r.at[h, 4 - i]), second_peer(h, i)).start()
 
         loop(1, 4, go)
+        loop(1, 4, go_on)
         q_all[h, 0, 0] = q_z[128 * h:128 * h + 128, :]
 
     def second(h):
-        arrived(q_all.at[h, 0, pl.ds(1, 3)], (s3.at[h, 0], s3.at[h, 1]))
-
-        def go(i):
-            remote(q_all.at[h, 0], q_all.at[h, 4 - i], (q4s.at[h], q4r.at[h, 4 - i]), second_peer(h, i)).start()
-
-        loop(1, 4, go)
+        def pass_on(j):
+            r = j + j // 2 - 2 * (j // 3)
+            arrived(q_all.at[h, 0, r], (s3.at[h, 0], s3.at[h, r]))
+
+            def go(i):
+                remote(q_all.at[h, 0, r], q_all.at[h, 4 - i, r], (q4s.at[h], q4r.at[h, 4 - i]), second_peer(h, i)).start()
+
+            loop(1, 4, go)
+
+        loop(1, 4, pass_on)
 
     arrived(q_z.at[pl.ds(0, 128)], pair(s1))
     remote(z_rows(5, 4), z_rows(9, 4), pair(s2), dev(x, y, z - 4, core)).start()
     remote(z_rows(1, 3), z_rows(13, 3), pair(s2), dev(x, y, z + 4, core)).start()
     first(0)
+
+    def spread(group, slot, to):
+        remote(features(k_ref, group), k_all.at[slot], (kv.at[0], kv.at[1]), to).start()
+        remote(features(v_ref, group), v_place(slot), (kv.at[2], kv.at[3]), to).start()
+
+    def spread_z(c):
+        for d, slot in ((1, 2 + core), (-1, 4 + core), (d2, 6 + core)):
+            spread(2 * ((u + d + 4) % 4) + c, slot, dev(x, y, z + d, c))
+
+    loop(0, 2, spread_z)
+    spread(2 * u + 1 - core, 1, other)
+
     loop(0, 32, spread_pos)
     second(0)
     arrived(z_rows(9, 7), pair(s2))
     first(1)
+    second(1)
 
     own_k.wait()
     own_v.wait()
@@ -215,23 +226,18 @@
     eye = lax.broadcasted_iota(jnp.int32, (HEAD, HEAD), 0) == lax.broadcasted_iota(jnp.int32, (HEAD, HEAD), 1)
 
     def chunk(i):
-        code = i - ((i + 6) // 8 - (i + 3) // 8) + 3 * ((i + 7) // 8 - (i + 6) // 8)
-        h, t = code // 4, code % 4
-
-        @pl.when(i == 1)
-        def _():
-            second(1)
-
-        @pl.when(i >= 2)
+        h, t = i // 4, i % 4
+
+        @pl.when(t > 0)
         def _():
             arrived(q_all.at[h, t], (q4s.at[h], q4r.at[h, t]))
 
-        def block(b):
-            q = q_all[h, t, b]
+        for b in (0, 2):
+            q = q_all[h, t, b:b + 2].reshape(256, HEAD)
             scores = lax.dot_general(
                 q, k_all[...].reshape(1024, HEAD), (((1,), (1,)), ((), ())), preferred_element_type=F32
             )
-            limit = thr[code * 4 + b]
+            limit = thr[pl.ds(4 * i + b, 2)].reshape(256, HEAD)
             parts = [
                 jnp.where(key_pos[j:j + 1, :] <= limit, scores[:, j * HEAD:(j + 1) * HEAD], HIDDEN) for j in range(8)
             ]
@@ -244,13 +250,14 @@
                 weights, v_all[...].reshape(1024, 2 * HEAD), (((1,), (0,)), ((), ())), preferred_element_type=F32
             )
             total = both[:, HEAD:]
-            o_all[h, t, b] = (both[:, :HEAD] / total).astype(BF16)
+            o_all[h, t, b:b + 2] = (both[:, :HEAD] / total).astype(BF16).reshape(2, HEAD, HEAD)
             level = top + jnp.log2(total)
-            l_all[h, t, pl.ds(b, 1), :] = jnp.sum(jnp.where(eye, level, 0.0), axis=0, keepdims=True)
-
-        loop(0, 4, block)
-
-        @pl.when(i >= 2)
+            for r in range(2):
+                l_all[h, t, b + r:b + r + 1, :] = jnp.sum(
+                    jnp.where(eye, level[r * HEAD:(r + 1) * HEAD], 0.0), axis=0, keepdims=True
+                )
+
+        @pl.when(t > 0)
         def _():
             to = second_peer(h, t)
             remote(o_all.at[h, t], o_in.at[h, 4 - t], (osn.at[h], orc.at[h]), to).start()
@@ -292,7 +299,7 @@
         lz_out[h] = level
 
         def go(i):
-            s = 8 * h + i
+            s = 8 * h + (i + 4 * h) % 8
 
             @pl.when(s != 4)
             def _():
@@ -376,7 +383,7 @@
             vmem((256, HEAD), BF16), vmem((2, 1, HEAD), F32),
             vmem((16, 16, HEAD), BF16), vmem((16, 1, HEAD), F32),
             vmem((4, 8, HEAD), F32), vmem((4, 8, HEAD), F32), vmem((8, 8, HEAD), F32),
-            dma((4,)), dma((2,)), dma((2,)), dma((2,)), dma((2, 2)), dma((2,)), dma((2, 4)), dma((4,)),
+            dma((4,)), dma((2,)), dma((2,)), dma((2,)), dma((2, 4)), dma((2,)), dma((2, 4)), dma((4,)),
             dma((2,)), dma((2,)), dma((2,)), dma((2,)), dma((2, 2)), dma((2, 2)), dma((2,)), dma((2,)), dma((2,)),
         ],
         compiler_params=pltpu.CompilerParams(

time: 71.2 us -> 63.7 us (0.89)
  Pallas kernels: 69.6 us -> 62.1 us
    pallas_call x1, Pallas kernels: 69.6 us -> 62.1 us  [per_device(): pl.pallas_call(kernel, out_shape=jax.ShapeDtypeStruct(queries.shape, BF16...]
where the time goes in v3:
time: 63.7 us; the launch traced here: 63.4 us
  Pallas kernels  62.1 us (97%)
  local copies, waits for them, and re-layouts  1.34 us (2%)
    pallas_call x1, Pallas kernels, per_device(): pl.pallas_call(kernel, out_shape=jax.ShapeDtypeStruct(queries.shape, BF16...  62.1 us
    unnamed x1, local copies, waits for them, and re-layouts  1.34 us

profile of v3, /device:TPU:1, one launch (start us, length us, event | category | flops | bytes accessed | tf_op | source)
XLA Modules:
  0.0 63.4 jit_solution(7199413975272512938)
XLA Ops:
  0.0 62.1 %shard_map.46 = bf16[2,4096]{1,0:T(2,128)(2,1)} custom-call(bf16[2,4096]{1,0:T(2,128)(2,1)} %q_ref.1, bf16[128,1024]{1,0:T(8,128)(2,1)} %k_ref.1, bf16[128,1024]{1,0:T(8,128)(2,1)} %v_ref.1, s32[16]{0:T(128)} %wb_ref.1), custom_call_target="tpu_custom_call" | custom-call | tf_op jit(solution)/shard_map/pallas_call | solution.py:369
  62.1 1.3 %copy.6 = bf16[2,4096]{1,0:T(2,128)(2,1)} copy(bf16[2,4096]{1,0:T(2,128)(2,1)} %shard_map.46) | data formatting | bytes 32768

commit v4 on v3

--- a/solution.py
+++ b/solution.py
@@ -38,7 +38,7 @@
     wb, q_own, q_f32, q_cls, q_z, q_all, k_all, v_all, pos, thr, key_pos,
     o_all, l_all, o_in, l_in, p_out, lp_out, p_in, lp_in,
     z_out, lz_out, z_in, lz_in, s_out, s_in, f_in,
-    own, swap, s1, s2, s3, q4s, q4r, kv, osn, orc, lsn, lrc, ps, lps, zs, lzs, fs,
+    own, swap, s1, s2, s3, s3r, q4s, q4r, kv, osn, orc, lsn, lrc, ps, lps, zs, lzs, fs,
 ):
     u = lax.axis_index("uly")
     row = lax.axis_index("row")
@@ -115,11 +115,11 @@
     own_k.start()
     own_v.start()
     v_all[:, :, HEAD:] = jnp.ones((8, HEAD, HEAD), BF16)
+    pl.semaphore_wait(barrier, 18)
+
+    remote(q_ref, q_own.at[1], pair(swap), other).start()
     own_q.wait()
     own_wb.wait()
-    pl.semaphore_wait(barrier, 18)
-
-    remote(q_ref, q_own.at[1], pair(swap), other).start()
     arrived(q_own.at[1], pair(swap))
 
     def pack(c):
@@ -144,11 +144,11 @@
 
     blk = lax.broadcasted_iota(jnp.int32, (32, HEAD), 0)
     lane = lax.broadcasted_iota(jnp.int32, (32, HEAD), 1)
-    half, step, sub = blk >> 4, (blk >> 2) & 3, blk & 3
-    ys = (y + jnp.where(half == 0, step, sub)) & 3
-    xs = (x + jnp.where(half == 0, sub, step)) & 3
+    half, step, side, sub = blk >> 4, (blk >> 2) & 3, (blk >> 1) & 1, 2 * (blk & 1) + (lane >> 6)
+    ys = (y + jnp.where(side == 0, step, sub)) & 3
+    xs = (x + jnp.where(side == 0, sub, step)) & 3
     cs = jnp.where((lane & 8) == 0, core, 1 - core)
-    z_src = (z + 8 * half + (lane >> 4) + 12) & 15
+    z_src = (z + 8 * half + 4 * side + ((lane >> 4) & 3) + 12) & 15
     which = 2 * (2 * xs + cs) + (z_src >> 3)
     block_at = jnp.zeros((32, HEAD), jnp.int32)
     for i in range(16):
@@ -165,34 +165,40 @@
     def spread_pos(b):
         thr[b] = expand(pos[pl.ds(b, 1), :])
 
-    def first_peer(h, i):
-        return dev(x + i * (1 - h), y + i * h, z, core)
-
-    def second_peer(h, i):
-        return dev(x + i * h, y + i * (1 - h), z, core)
+    def first_peer(a, i):
+        return dev(x + i * (1 - a), y + i * a, z, core)
+
+    def second_peer(a, i):
+        return dev(x + i * a, y + i * (1 - a), z, core)
 
     def first(h):
-        mine = q_z.at[pl.ds(128 * h, 128)]
-
-        def go(i):
-            remote(mine, q_all.at[h, 0, 4 - i], (s3.at[h, 0], s3.at[h, 4 - i]), first_peer(h, i)).start()
-
-        def go_on(i):
-            remote(mine, q_all.at[h, 4 - i, 0], (q4s.at[h], q4r.at[h, 4 - i]), second_peer(h, i)).start()
-
-        loop(1, 4, go)
-        loop(1, 4, go_on)
-        q_all[h, 0, 0] = q_z[128 * h:128 * h + 128, :]
+        for a in range(2):
+            mine = q_z.at[pl.ds(128 * h + 64 * a, 64)]
+
+            def go(i):
+                remote(mine, q_all.at[h, 0, a, 4 - i], (s3.at[h], s3r.at[h, a, 4 - i]), first_peer(a, i)).start()
+
+            loop(1, 4, go)
+        for a in range(2):
+            mine = q_z.at[pl.ds(128 * h + 64 * a, 64)]
+
+            def go_on(i):
+                remote(mine, q_all.at[h, 4 - i, a, 0], (q4s.at[h], q4r.at[h, 4 - i]), second_peer(a, i)).start()
+
+            loop(1, 4, go_on)
+            q_all[h, 0, a, 0] = q_z[128 * h + 64 * a:128 * h + 64 * a + 64, :]
 
     def second(h):
         def pass_on(j):
             r = j + j // 2 - 2 * (j // 3)
-            arrived(q_all.at[h, 0, r], (s3.at[h, 0], s3.at[h, r]))
-
-            def go(i):
-                remote(q_all.at[h, 0, r], q_all.at[h, 4 - i, r], (q4s.at[h], q4r.at[h, 4 - i]), second_peer(h, i)).start()
-
-            loop(1, 4, go)
+            for a in range(2):
+                block = q_all.at[h, 0, a, r]
+                arrived(block, (s3.at[h], s3r.at[h, a, r]))
+
+                def go(i):
+                    remote(block, q_all.at[h, 4 - i, a, r], (q4s.at[h], q4r.at[h, 4 - i]), second_peer(a, i)).start()
+
+                loop(1, 4, go)
 
         loop(1, 4, pass_on)
 
@@ -232,12 +238,12 @@
         def _():
             arrived(q_all.at[h, t], (q4s.at[h], q4r.at[h, t]))
 
-        for b in (0, 2):
-            q = q_all[h, t, b:b + 2].reshape(256, HEAD)
+        for a in range(2):
+            q = q_all[h, t, a].reshape(256, HEAD)
             scores = lax.dot_general(
                 q, k_all[...].reshape(1024, HEAD), (((1,), (1,)), ((), ())), preferred_element_type=F32
             )
-            limit = thr[pl.ds(4 * i + b, 2)].reshape(256, HEAD)
+            limit = thr[pl.ds(4 * i + 2 * a, 2)].reshape(256, HEAD)
             parts = [
                 jnp.where(key_pos[j:j + 1, :] <= limit, scores[:, j * HEAD:(j + 1) * HEAD], HIDDEN) for j in range(8)
             ]
@@ -250,18 +256,19 @@
                 weights, v_all[...].reshape(1024, 2 * HEAD), (((1,), (0,)), ((), ())), preferred_element_type=F32
             )
             total = both[:, HEAD:]
-            o_all[h, t, b:b + 2] = (both[:, :HEAD] / total).astype(BF16).reshape(2, HEAD, HEAD)
+            o_all[h, t, a] = (both[:, :HEAD] / total).astype(BF16).reshape(2, HEAD, HEAD)
             level = top + jnp.log2(total)
             for r in range(2):
-                l_all[h, t, b + r:b + r + 1, :] = jnp.sum(
+                l_all[h, t, a, r:r + 1, :] = jnp.sum(
                     jnp.where(eye, level[r * HEAD:(r + 1) * HEAD], 0.0), axis=0, keepdims=True
                 )
 
         @pl.when(t > 0)
         def _():
-            to = second_peer(h, t)
-            remote(o_all.at[h, t], o_in.at[h, 4 - t], (osn.at[h], orc.at[h]), to).start()
-            remote(l_all.at[h, t], l_in.at[h, 4 - t], (lsn.at[h], lrc.at[h]), to).start()
+            for a in range(2):
+                to = second_peer(a, t)
+                remote(o_all.at[h, t, a], o_in.at[h, 4 - t, a], (osn.at[h], orc.at[h]), to).start()
+                remote(l_all.at[h, t, a], l_in.at[h, 4 - t, a], (lsn.at[h], lrc.at[h]), to).start()
 
     loop(0, 8, chunk)
 
@@ -270,17 +277,21 @@
         arrived(l_in.at[h, pl.ds(1, 3)], (lsn.at[h], lrc.at[h]))
 
         def block(i):
-            b = (i + 1) % 4
-            level, shares = combine([l_all[h, 0, pl.ds(b, 1), :]] + [l_in[h, t, pl.ds(b, 1), :] for t in range(1, 4)])
-            values = [o_all[h, 0, b]] + [o_in[h, t, b] for t in range(1, 4)]
-            p_out[h, b] = weighted([expand(share) for share in shares], values).astype(BF16)
-            lp_out[h, b] = level
-
-            @pl.when(i < 3)
-            def _():
-                to = first_peer(h, b)
-                remote(p_out.at[h, b], p_in.at[h, 4 - b], (ps.at[h, 0], ps.at[h, 1]), to).start()
-                remote(lp_out.at[h, b], lp_in.at[h, 4 - b], (lps.at[h, 0], lps.at[h, 1]), to).start()
+            a, k = i % 2, 1 - i // 2
+            levels = [l_all[h, 0, a, pl.ds(k, 1), :]] + [l_in[h, t, a, pl.ds(k, 1), :] for t in range(1, 4)]
+            level, shares = combine(levels)
+            values = [o_all[h, 0, a, k]] + [o_in[h, t, a, k] for t in range(1, 4)]
+            joined = weighted([expand(share) for share in shares], values).astype(BF16)
+            lp_out[h, a, k] = level
+            for m in range(2):
+                sub = 2 * k + m
+                p_out[h, sub, a] = joined[64 * m:64 * m + 64]
+
+                @pl.when(sub > 0)
+                def _():
+                    to = first_peer(a, sub)
+                    remote(p_out.at[h, sub, a], p_in.at[h, 4 - sub, a], (ps.at[h, 0], ps.at[h, 1]), to).start()
+                    remote(lp_out.at[h, a, k], lp_in.at[h, 4 - sub, a], (lps.at[h, 0], lps.at[h, 1]), to).start()
 
         loop(0, 4, block)
 
@@ -288,12 +299,18 @@
 
     def z_part(ref, s):
         return ref.at[pl.ds(pl.multiple_of(16 * s, 16), 16)]
+
+    low = lax.broadcasted_iota(jnp.int32, (1, HEAD), 1) < 64
 
     def join_first(h):
         arrived(p_in.at[h, pl.ds(1, 3)], (ps.at[h, 0], ps.at[h, 1]))
         arrived(lp_in.at[h, pl.ds(1, 3)], (lps.at[h, 0], lps.at[h, 1]))
-        level, shares = combine([lp_out[h, 0]] + [lp_in[h, b] for b in range(1, 4)])
-        values = [p_out[h, 0]] + [p_in[h, b] for b in range(1, 4)]
+        levels = [jnp.where(low, lp_out[h, 0, 0], pltpu.roll(lp_out[h, 1, 0], 64, 1))]
+        levels.append(jnp.where(low, pltpu.roll(lp_in[h, 1, 0], 64, 1), lp_in[h, 1, 1]))
+        levels.append(jnp.where(low, lp_in[h, 2, 0], pltpu.roll(lp_in[h, 2, 1], 64, 1)))
+        levels.append(jnp.where(low, pltpu.roll(lp_in[h, 3, 0], 64, 1), lp_in[h, 3, 1]))
+        level, shares = combine(levels)
+        values = [part.reshape(HEAD, HEAD) for part in [p_out[h, 0]] + [p_in[h, b] for b in range(1, 4)]]
         joined = weighted([expand(share) for share in shares], values).astype(BF16)
         z_out[pl.ds(pl.multiple_of(128 * h, 128), 128), :] = joined
         lz_out[h] = level
@@ -352,7 +369,7 @@
     sent(k_all.at[pl.ds(1, 7)], (kv.at[0], kv.at[1]))
     sent(v_all.at[pl.ds(1, 7), :, pl.ds(0, HEAD)], (kv.at[2], kv.at[3]))
     for h in range(2):
-        sent(q_all.at[h, 0, pl.ds(1, 3)], (s3.at[h, 0], s3.at[h, 1]))
+        sent(q_all.at[h, 0, :, pl.ds(1, 3)], (s3.at[h], s3.at[h]))
         sent(q_all.at[h, pl.ds(1, 3)], (q4s.at[h], q4r.at[h, 0]))
         sent(o_in.at[h, pl.ds(1, 3)], (osn.at[h], orc.at[h]))
         sent(l_in.at[h, pl.ds(1, 3)], (lsn.at[h], lrc.at[h]))
@@ -374,16 +391,16 @@
         scratch_shapes=[
             pltpu.SMEM((16,), jnp.int32),
             vmem((2, 2, 4096), BF16), vmem((4, 16, HEAD), F32), vmem((4, 16, HEAD), BF16), vmem((256, HEAD), BF16),
-            vmem((2, 4, 4, HEAD, HEAD), BF16), vmem((8, HEAD, HEAD), BF16), vmem((8, HEAD, 2 * HEAD), BF16),
+            vmem((2, 4, 2, 4, 64, HEAD), BF16), vmem((8, HEAD, HEAD), BF16), vmem((8, HEAD, 2 * HEAD), BF16),
             vmem((32, HEAD), F32), vmem((32, HEAD, HEAD), F32), vmem((8, HEAD), F32),
-            vmem((2, 4, 4, HEAD, HEAD), BF16), vmem((2, 4, 4, HEAD), F32),
-            vmem((2, 4, 4, HEAD, HEAD), BF16), vmem((2, 4, 4, HEAD), F32),
-            vmem((2, 4, HEAD, HEAD), BF16), vmem((2, 4, 1, HEAD), F32),
-            vmem((2, 4, HEAD, HEAD), BF16), vmem((2, 4, 1, HEAD), F32),
+            vmem((2, 4, 2, 2, HEAD, HEAD), BF16), vmem((2, 4, 2, 2, HEAD), F32),
+            vmem((2, 4, 2, 2, HEAD, HEAD), BF16), vmem((2, 4, 2, 2, HEAD), F32),
+            vmem((2, 4, 2, 64, HEAD), BF16), vmem((2, 2, 2, 1, HEAD), F32),
+            vmem((2, 4, 2, 64, HEAD), BF16), vmem((2, 4, 2, 1, HEAD), F32),
             vmem((256, HEAD), BF16), vmem((2, 1, HEAD), F32),
             vmem((16, 16, HEAD), BF16), vmem((16, 1, HEAD), F32),
             vmem((4, 8, HEAD), F32), vmem((4, 8, HEAD), F32), vmem((8, 8, HEAD), F32),
-            dma((4,)), dma((2,)), dma((2,)), dma((2,)), dma((2, 4)), dma((2,)), dma((2, 4)), dma((4,)),
+            dma((4,)), dma((2,)), dma((2,)), dma((2,)), dma((2,)), dma((2, 2, 4)), dma((2,)), dma((2, 4)), dma((4,)),
             dma((2,)), dma((2,)), dma((2,)), dma((2,)), dma((2, 2)), dma((2, 2)), dma((2,)), dma((2,)), dma((2,)),
         ],
         compiler_params=pltpu.CompilerParams(

time: 63.7 us -> 59.8 us (0.939)
  Pallas kernels: 62.1 us -> 58.3 us
    pallas_call x1, Pallas kernels: 62.1 us -> 58.3 us  [per_device(): pl.pallas_call(kernel, out_shape=jax.ShapeDtypeStruct(queries.shape, BF16...]
where the time goes in v4:
time: 59.8 us; the launch traced here: 59.6 us
  Pallas kernels  58.3 us (97%)
  local copies, waits for them, and re-layouts  1.34 us (2%)
    pallas_call x1, Pallas kernels, per_device(): pl.pallas_call(kernel, out_shape=jax.ShapeDtypeStruct(queries.shape, BF16...  58.3 us
    unnamed x1, local copies, waits for them, and re-layouts  1.34 us

profile of v4, /device:TPU:1, one launch (start us, length us, event | category | flops | bytes accessed | tf_op | source)
XLA Modules:
  0.0 59.6 jit_solution(2362222867342220629)
XLA Ops:
  0.0 58.3 %shard_map.46 = bf16[2,4096]{1,0:T(2,128)(2,1)} custom-call(bf16[2,4096]{1,0:T(2,128)(2,1)} %q_ref.1, bf16[128,1024]{1,0:T(8,128)(2,1)} %k_ref.1, bf16[128,1024]{1,0:T(8,128)(2,1)} %v_ref.1, s32[16]{0:T(128)} %wb_ref.1), custom_call_target="tpu_custom_call" | custom-call | tf_op jit(solution)/shard_map/pallas_call | solution.py:386
  58.3 1.3 %copy.6 = bf16[2,4096]{1,0:T(2,128)(2,1)} copy(bf16[2,4096]{1,0:T(2,128)(2,1)} %shard_map.46) | data formatting | bytes 32768

commit v5 on v3

--- a/solution.py
+++ b/solution.py
@@ -21,9 +21,8 @@
 def combine(levels):
     top = jnp.maximum(jnp.maximum(levels[0], levels[1]), jnp.maximum(levels[2], levels[3]))
     shares = [jnp.exp2(level - top) for level in levels]
-    total = (shares[0] + shares[1]) + (shares[2] + shares[3])
-    inverse = 1.0 / total
-    return top + jnp.log2(total), [share * inverse for share in shares]
+    inverse = 1.0 / ((shares[0] + shares[1]) + (shares[2] + shares[3]))
+    return [share * inverse for share in shares]
 
 
 def weighted(shares, values):
@@ -36,9 +35,9 @@
 def kernel(
     q_ref, k_ref, v_ref, wb_ref, out_ref,
     wb, q_own, q_f32, q_cls, q_z, q_all, k_all, v_all, pos, thr, key_pos,
-    o_all, l_all, o_in, l_in, p_out, lp_out, p_in, lp_in,
+    o_all, l_all, o_in, l_in,
     z_out, lz_out, z_in, lz_in, s_out, s_in, f_in,
-    own, swap, s1, s2, s3, q4s, q4r, kv, osn, orc, lsn, lrc, ps, lps, zs, lzs, fs,
+    own, swap, s1, s2, qs, qr, kv, osn, orc, lsn, lrc, zs, lzs, fs,
 ):
     u = lax.axis_index("uly")
     row = lax.axis_index("row")
@@ -88,12 +87,17 @@
         greet(dev(x, y, z + 5 - j, core))
         greet(dev(x, y, z - 5 + j, core))
 
-    def greet_xy(i):
-        greet(dev(x + i, y, z, core))
-        greet(dev(x, y + i, z, core))
+    def at_plane(n):
+        return dev(x + n % 4, y + n // 4, z, core)
+
+    def back(n):
+        return (4 - n % 4) % 4 + 4 * ((4 - n // 4) % 4)
+
+    def greet_plane(n):
+        greet(at_plane(n))
 
     loop(1, 5, greet_z)
-    loop(1, 4, greet_xy)
+    loop(1, 16, greet_plane)
     greet(dev(x, y, z + 1, 1 - core))
     greet(dev(x, y, z - 1, 1 - core))
     greet(dev(x, y, z + d2, 1 - core))
@@ -115,11 +119,11 @@
     own_k.start()
     own_v.start()
     v_all[:, :, HEAD:] = jnp.ones((8, HEAD, HEAD), BF16)
+    pl.semaphore_wait(barrier, 27)
+
+    remote(q_ref, q_own.at[1], pair(swap), other).start()
     own_q.wait()
     own_wb.wait()
-    pl.semaphore_wait(barrier, 18)
-
-    remote(q_ref, q_own.at[1], pair(swap), other).start()
     arrived(q_own.at[1], pair(swap))
 
     def pack(c):
@@ -144,9 +148,7 @@
 
     blk = lax.broadcasted_iota(jnp.int32, (32, HEAD), 0)
     lane = lax.broadcasted_iota(jnp.int32, (32, HEAD), 1)
-    half, step, sub = blk >> 4, (blk >> 2) & 3, blk & 3
-    ys = (y + jnp.where(half == 0, step, sub)) & 3
-    xs = (x + jnp.where(half == 0, sub, step)) & 3
+    half, ys, xs = blk >> 4, (y + (blk >> 2)) & 3, (x + blk) & 3
     cs = jnp.where((lane & 8) == 0, core, 1 - core)
     z_src = (z + 8 * half + (lane >> 4) + 12) & 15
     which = 2 * (2 * xs + cs) + (z_src >> 3)
@@ -165,41 +167,23 @@
     def spread_pos(b):
         thr[b] = expand(pos[pl.ds(b, 1), :])
 
-    def first_peer(h, i):
-        return dev(x + i * (1 - h), y + i * h, z, core)
-
-    def second_peer(h, i):
-        return dev(x + i * h, y + i * (1 - h), z, core)
-
-    def first(h):
-        mine = q_z.at[pl.ds(128 * h, 128)]
-
-        def go(i):
-            remote(mine, q_all.at[h, 0, 4 - i], (s3.at[h, 0], s3.at[h, 4 - i]), first_peer(h, i)).start()
-
-        def go_on(i):
-            remote(mine, q_all.at[h, 4 - i, 0], (q4s.at[h], q4r.at[h, 4 - i]), second_peer(h, i)).start()
-
-        loop(1, 4, go)
-        loop(1, 4, go_on)
-        q_all[h, 0, 0] = q_z[128 * h:128 * h + 128, :]
-
-    def second(h):
-        def pass_on(j):
-            r = j + j // 2 - 2 * (j // 3)
-            arrived(q_all.at[h, 0, r], (s3.at[h, 0], s3.at[h, r]))
-
-            def go(i):
-                remote(q_all.at[h, 0, r], q_all.at[h, 4 - i, r], (q4s.at[h], q4r.at[h, 4 - i]), second_peer(h, i)).start()
-
-            loop(1, 4, go)
-
-        loop(1, 4, pass_on)
+    def turn(j):
+        return j + j // 2 - 2 * (j // 3)
+
+    def gather(h):
+        def go(j):
+            n = 4 * ((4 - turn(j // 4)) % 4) + j % 4
+            there = back(n)
+            to = (qs.at[h], qr.at[h, there // 4])
+            remote(q_z.at[pl.ds(128 * h, 128)], q_all.at[h, there], to, at_plane(n)).start()
+
+        loop(1, 16, go)
+        q_all[h, 0] = q_z[128 * h:128 * h + 128, :]
 
     arrived(q_z.at[pl.ds(0, 128)], pair(s1))
     remote(z_rows(5, 4), z_rows(9, 4), pair(s2), dev(x, y, z - 4, core)).start()
     remote(z_rows(1, 3), z_rows(13, 3), pair(s2), dev(x, y, z + 4, core)).start()
-    first(0)
+    gather(0)
 
     def spread(group, slot, to):
         remote(features(k_ref, group), k_all.at[slot], (kv.at[0], kv.at[1]), to).start()
@@ -213,10 +197,8 @@
     spread(2 * u + 1 - core, 1, other)
 
     loop(0, 32, spread_pos)
-    second(0)
     arrived(z_rows(9, 7), pair(s2))
-    first(1)
-    second(1)
+    gather(1)
 
     own_k.wait()
     own_v.wait()
@@ -226,18 +208,23 @@
     eye = lax.broadcasted_iota(jnp.int32, (HEAD, HEAD), 0) == lax.broadcasted_iota(jnp.int32, (HEAD, HEAD), 1)
 
     def chunk(i):
-        h, t = i // 4, i % 4
+        h, t = i // 4, turn(i % 4)
+
+        @pl.when(t == 0)
+        def _():
+            arrived(q_all.at[h, pl.ds(1, 3)], (qs.at[h], qr.at[h, 0]))
 
         @pl.when(t > 0)
         def _():
-            arrived(q_all.at[h, t], (q4s.at[h], q4r.at[h, t]))
-
-        for b in (0, 2):
-            q = q_all[h, t, b:b + 2].reshape(256, HEAD)
+            arrived(q_all.at[h, pl.ds(4 * t, 4)], (qs.at[h], qr.at[h, t]))
+
+        for a in range(2):
+            n = 4 * t + 2 * a
+            q = q_all[h, pl.ds(n, 2)].reshape(256, HEAD)
             scores = lax.dot_general(
                 q, k_all[...].reshape(1024, HEAD), (((1,), (1,)), ((), ())), preferred_element_type=F32
             )
-            limit = thr[pl.ds(4 * i + b, 2)].reshape(256, HEAD)
+            limit = thr[pl.ds(16 * h + n, 2)].reshape(256, HEAD)
             parts = [
                 jnp.where(key_pos[j:j + 1, :] <= limit, scores[:, j * HEAD:(j + 1) * HEAD], HIDDEN) for j in range(8)
             ]
@@ -250,53 +237,51 @@
                 weights, v_all[...].reshape(1024, 2 * HEAD), (((1,), (0,)), ((), ())), preferred_element_type=F32
             )
             total = both[:, HEAD:]
-            o_all[h, t, b:b + 2] = (both[:, :HEAD] / total).astype(BF16).reshape(2, HEAD, HEAD)
+            o_all[h, pl.ds(n, 2)] = (both[:, :HEAD] / total).astype(BF16).reshape(2, HEAD, HEAD)
             level = top + jnp.log2(total)
             for r in range(2):
-                l_all[h, t, b + r:b + r + 1, :] = jnp.sum(
+                l_all[h, n + r] = jnp.sum(
                     jnp.where(eye, level[r * HEAD:(r + 1) * HEAD], 0.0), axis=0, keepdims=True
                 )
 
-        @pl.when(t > 0)
-        def _():
-            to = second_peer(h, t)
-            remote(o_all.at[h, t], o_in.at[h, 4 - t], (osn.at[h], orc.at[h]), to).start()
-            remote(l_all.at[h, t], l_in.at[h, 4 - t], (lsn.at[h], lrc.at[h]), to).start()
+        def go(m):
+            n = 4 * t + m
+
+            @pl.when(n > 0)
+            def _():
+                to = at_plane(n)
+                remote(o_all.at[h, n], o_in.at[h, back(n)], (osn.at[h], orc.at[h]), to).start()
+                remote(l_all.at[h, n], l_in.at[h, back(n)], (lsn.at[h], lrc.at[h]), to).start()
+
+        loop(0, 4, go)
 
     loop(0, 8, chunk)
-
-    def join_second(h):
-        arrived(o_in.at[h, pl.ds(1, 3)], (osn.at[h], orc.at[h]))
-        arrived(l_in.at[h, pl.ds(1, 3)], (lsn.at[h], lrc.at[h]))
-
-        def block(i):
-            b = (i + 1) % 4
-            level, shares = combine([l_all[h, 0, pl.ds(b, 1), :]] + [l_in[h, t, pl.ds(b, 1), :] for t in range(1, 4)])
-            values = [o_all[h, 0, b]] + [o_in[h, t, b] for t in range(1, 4)]
-            p_out[h, b] = weighted([expand(share) for share in shares], values).astype(BF16)
-            lp_out[h, b] = level
-
-            @pl.when(i < 3)
-            def _():
-                to = first_peer(h, b)
-                remote(p_out.at[h, b], p_in.at[h, 4 - b], (ps.at[h, 0], ps.at[h, 1]), to).start()
-                remote(lp_out.at[h, b], lp_in.at[h, 4 - b], (lps.at[h, 0], lps.at[h, 1]), to).start()
-
-        loop(0, 4, block)
-
-    loop(0, 2, join_second)
 
     def z_part(ref, s):
         return ref.at[pl.ds(pl.multiple_of(16 * s, 16), 16)]
 
-    def join_first(h):
-        arrived(p_in.at[h, pl.ds(1, 3)], (ps.at[h, 0], ps.at[h, 1]))
-        arrived(lp_in.at[h, pl.ds(1, 3)], (lps.at[h, 0], lps.at[h, 1]))
-        level, shares = combine([lp_out[h, 0]] + [lp_in[h, b] for b in range(1, 4)])
-        values = [p_out[h, 0]] + [p_in[h, b] for b in range(1, 4)]
-        joined = weighted([expand(share) for share in shares], values).astype(BF16)
-        z_out[pl.ds(pl.multiple_of(128 * h, 128), 128), :] = joined
+    def join(h):
+        o_in[h, 0] = o_all[h, 0]
+        l_in[h, 0] = l_all[h, 0]
+        arrived(l_in.at[h, pl.ds(1, 15)], (lsn.at[h], lrc.at[h]))
+        top = l_in[h, 0]
+        for n in range(1, 16):
+            top = jnp.maximum(top, l_in[h, n])
+        total = jnp.exp2(l_in[h, 0] - top)
+        for n in range(1, 16):
+            total = total + jnp.exp2(l_in[h, n] - top)
+        level = top + jnp.log2(total)
         lz_out[h] = level
+        arrived(o_in.at[h, pl.ds(1, 15)], (osn.at[h], orc.at[h]))
+
+        def add(i, acc):
+            for m in range(4):
+                n = 4 * i + m
+                acc = acc + expand(jnp.exp2(l_in[h, n] - level)) * o_in[h, n].astype(F32)
+            return acc
+
+        joined = lax.fori_loop(0, 4, add, jnp.zeros((HEAD, HEAD), F32))
+        z_out[pl.ds(pl.multiple_of(128 * h, 128), 128), :] = joined.astype(BF16)
 
         def go(i):
             s = 8 * h + (i + 4 * h) % 8
@@ -310,7 +295,7 @@
 
         loop(0, 8, go)
 
-    loop(0, 2, join_first)
+    loop(0, 2, join)
     z_in[0] = z_out[64:80, :]
     lz_in[0] = lz_out[0]
     arrived(z_in.at[pl.ds(1, 15)], pair(zs))
@@ -325,7 +310,7 @@
             wide = jnp.broadcast_to(lz_in[at], (16, HEAD))
             levels.append(jnp.sum(jnp.where(lane16 == offset, wide, 0.0), axis=1, keepdims=True))
             values.append(z_in[at])
-        _, shares = combine(levels)
+        shares = combine(levels)
         joined = weighted(shares, values)
         f_in[2 * ((u + w) % 4) + core] = joined[:8]
         s_out[w] = joined[8:]
@@ -352,12 +337,9 @@
     sent(k_all.at[pl.ds(1, 7)], (kv.at[0], kv.at[1]))
     sent(v_all.at[pl.ds(1, 7), :, pl.ds(0, HEAD)], (kv.at[2], kv.at[3]))
     for h in range(2):
-        sent(q_all.at[h, 0, pl.ds(1, 3)], (s3.at[h, 0], s3.at[h, 1]))
-        sent(q_all.at[h, pl.ds(1, 3)], (q4s.at[h], q4r.at[h, 0]))
-        sent(o_in.at[h, pl.ds(1, 3)], (osn.at[h], orc.at[h]))
-        sent(l_in.at[h, pl.ds(1, 3)], (lsn.at[h], lrc.at[h]))
-        sent(p_in.at[h, pl.ds(1, 3)], (ps.at[h, 0], ps.at[h, 1]))
-        sent(lp_in.at[h, pl.ds(1, 3)], (lps.at[h, 0], lps.at[h, 1]))
+        sent(q_all.at[h, pl.ds(1, 15)], (qs.at[h], qr.at[h, 0]))
+        sent(o_in.at[h, pl.ds(1, 15)], (osn.at[h], orc.at[h]))
+        sent(l_in.at[h, pl.ds(1, 15)], (lsn.at[h], lrc.at[h]))
     sent(z_in.at[pl.ds(1, 15)], pair(zs))
     sent(lz_in.at[pl.ds(1, 15)], pair(lzs))
     sent(s_in, pair(fs))
@@ -374,17 +356,15 @@
         scratch_shapes=[
             pltpu.SMEM((16,), jnp.int32),
             vmem((2, 2, 4096), BF16), vmem((4, 16, HEAD), F32), vmem((4, 16, HEAD), BF16), vmem((256, HEAD), BF16),
-            vmem((2, 4, 4, HEAD, HEAD), BF16), vmem((8, HEAD, HEAD), BF16), vmem((8, HEAD, 2 * HEAD), BF16),
+            vmem((2, 16, HEAD, HEAD), BF16), vmem((8, HEAD, HEAD), BF16), vmem((8, HEAD, 2 * HEAD), BF16),
             vmem((32, HEAD), F32), vmem((32, HEAD, HEAD), F32), vmem((8, HEAD), F32),
-            vmem((2, 4, 4, HEAD, HEAD), BF16), vmem((2, 4, 4, HEAD), F32),
-            vmem((2, 4, 4, HEAD, HEAD), BF16), vmem((2, 4, 4, HEAD), F32),
-            vmem((2, 4, HEAD, HEAD), BF16), vmem((2, 4, 1, HEAD), F32),
-            vmem((2, 4, HEAD, HEAD), BF16), vmem((2, 4, 1, HEAD), F32),
+            vmem((2, 16, HEAD, HEAD), BF16), vmem((2, 16, 1, HEAD), F32),
+            vmem((2, 16, HEAD, HEAD), BF16), vmem((2, 16, 1, HEAD), F32),
             vmem((256, HEAD), BF16), vmem((2, 1, HEAD), F32),
             vmem((16, 16, HEAD), BF16), vmem((16, 1, HEAD), F32),
             vmem((4, 8, HEAD), F32), vmem((4, 8, HEAD), F32), vmem((8, 8, HEAD), F32),
-            dma((4,)), dma((2,)), dma((2,)), dma((2,)), dma((2, 4)), dma((2,)), dma((2, 4)), dma((4,)),
-            dma((2,)), dma((2,)), dma((2,)), dma((2,)), dma((2, 2)), dma((2, 2)), dma((2,)), dma((2,)), dma((2,)),
+            dma((4,)), dma((2,)), dma((2,)), dma((2,)), dma((2,)), dma((2, 4)), dma((4,)),
+            dma((2,)), dma((2,)), dma((2,)), dma((2,)), dma((2,)), dma((2,)), dma((2,)),
         ],
         compiler_params=pltpu.CompilerParams(
             collective_id=0, has_side_effects=True, vmem_limit_bytes=58 * 1024 * 1024

time: 63.7 us -> 60.1 us (0.943)
  Pallas kernels: 62.1 us -> 58.5 us
    pallas_call x1, Pallas kernels: 62.1 us -> 58.5 us  [per_device(): pl.pallas_call(kernel, out_shape=jax.ShapeDtypeStruct(queries.shape, BF16...]
where the time goes in v5:
time: 60.1 us; the launch traced here: 59.9 us
  Pallas kernels  58.5 us (97%)
  local copies, waits for them, and re-layouts  1.34 us (2%)
    pallas_call x1, Pallas kernels, per_device(): pl.pallas_call(kernel, out_shape=jax.ShapeDtypeStruct(queries.shape, BF16...  58.5 us
    unnamed x1, local copies, waits for them, and re-layouts  1.34 us

profile of v5, /device:TPU:1, one launch (start us, length us, event | category | flops | bytes accessed | tf_op | source)
XLA Modules:
  0.0 59.9 jit_solution(15310979357407463351)
XLA Ops:
  0.0 58.5 %shard_map.46 = bf16[2,4096]{1,0:T(2,128)(2,1)} custom-call(bf16[2,4096]{1,0:T(2,128)(2,1)} %q_ref.1, bf16[128,1024]{1,0:T(8,128)(2,1)} %k_ref.1, bf16[128,1024]{1,0:T(8,128)(2,1)} %v_ref.1, s32[16]{0:T(128)} %wb_ref.1), custom_call_target="tpu_custom_call" | custom-call | tf_op jit(solution)/shard_map/pallas_call | solution.py:351
  58.5 1.3 %copy.6 = bf16[2,4096]{1,0:T(2,128)(2,1)} copy(bf16[2,4096]{1,0:T(2,128)(2,1)} %shard_map.46) | data formatting | bytes 32768

commit v6 on v4

v6 whole, which is shorter than its diff:
```python
import math

import jax
import jax.numpy as jnp
from jax import lax
from jax.experimental import pallas as pl
from jax.experimental.pallas import tpu as pltpu
from jax.sharding import PartitionSpec as P

HEAD = 128
MESH = pl.DeviceIdType.MESH
SCALE = math.log2(math.e) / math.sqrt(HEAD)
HIDDEN = -1e30
F32, BF16 = jnp.float32, jnp.bfloat16


def expand(row):
    return jnp.transpose(jnp.broadcast_to(row, (HEAD, HEAD)))


def combine(levels):
    top = jnp.maximum(jnp.maximum(levels[0], levels[1]), jnp.maximum(levels[2], levels[3]))
    shares = [jnp.exp2(level - top) for level in levels]
    total = (shares[0] + shares[1]) + (shares[2] + shares[3])
    inverse = 1.0 / total
    return top + jnp.log2(total), [share * inverse for share in shares]


def weighted(shares, values):
    acc = shares[0] * values[0].astype(F32)
    for share, value in zip(shares[1:], values[1:]):
        acc = acc + share * value.astype(F32)
    return acc


def kernel(
    q_ref, k_ref, v_ref, wb_ref, out_ref,
    wb, q_own, q_f32, q_cls, q_z, q_all, k_all, v_all, pos, thr, key_pos,
    o_all, l_all, o_in, l_in, p_out, lp_out, p_in, lp_in, ob_in, lb_in, share_b,
    z_out, lz_out, z_in, lz_in, s_out, s_in, f_in,
    own, swap, s1, s2, s3, s3r, q4s, q4r, kv, os, ls, ps, lps, obs, lbs, zs, lzs, fs,
):
    u = lax.axis_index("uly")
    row = lax.axis_index("row")
    col = lax.axis_index("col")
    rem, div = lax.rem, lax.div
    x, core = div(row, 2), rem(row, 2)
    y, z_high = rem(col, 4), div(col, 4)
    z = z_high * 4 + u

    def along(d, core_at):
        z_at = rem(z + (d + 16), 16)
        return {"uly": rem(z_at, 4), "row": 2 * x + core_at, "col": div(z_at, 4) * 4 + y}

    def plane(dx, dy):
        return {"uly": u, "row": 2 * rem(x + dx, 4) + core, "col": 4 * z_high + rem(y + dy, 4)}

    def remote(src, dst, sems, to):
        return pltpu.make_async_remote_copy(
            src_ref=src, dst_ref=dst, send_sem=sems[0], recv_sem=sems[1], device_id=to, device_id_type=MESH
        )

    other = {"uly": u, "row": 2 * x + 1 - core, "col": col}

    def pair(sem):
        return sem.at[0], sem.at[1]

    def arrived(ref, sems):
        remote(ref, ref, sems, other).wait_recv()

    def sent(ref, sems):
        remote(ref, ref, sems, other).wait_send()

    def loop(start, stop, body):
        def step(i, carry):
            body(i)
            return carry

        lax.fori_loop(start, stop, step, 0)

    d2 = 2 - 4 * core
    barrier = pltpu.get_barrier_semaphore()

    def greet(to):
        pl.semaphore_signal(barrier, inc=1, device_id=to, device_id_type=MESH)

    for d in (4, -4, 3, -3, 2, -2, 1, -1):
        greet(along(d, core))
    for i in (2, 1, 3):
        greet(plane(i, 0))
        greet(plane(0, i))
    for d in (d2, 1, -1):
        greet(along(d, 1 - core))
    greet(other)
    own_q = pltpu.make_async_copy(q_ref, q_own.at[0], own.at[0])
    own_q.start()
    own_wb = pltpu.make_async_copy(wb_ref, wb, own.at[1])
    own_wb.start()

    def features(ref, group):
        return ref.at[:, pl.ds(pl.multiple_of(group * HEAD, HEAD), HEAD)]

    def v_place(slot):
        return v_all.at[slot, :, pl.ds(0, HEAD)]

    my_group = 2 * u + core
    own_k = pltpu.make_async_copy(features(k_ref, my_group), k_all.at[0], own.at[2])
    own_v = pltpu.make_async_copy(features(v_ref, my_group), v_place(0), own.at[3])
    own_k.start()
    own_v.start()
    v_all[:, :, HEAD:] = jnp.ones((8, HEAD, HEAD), BF16)
    pl.semaphore_wait(barrier, 18)

    remote(q_ref, q_own.at[1], pair(swap), other).start()
    own_q.wait()
    own_wb.wait()
    arrived(q_own.at[1], pair(swap))

    def pack(c):
        for r in range(2):
            for g in range(4):
                at = pl.multiple_of(((2 * c + core) * 4 + g) * HEAD, HEAD)
                q_f32[c, 8 * r + 2 * g:8 * r + 2 * g + 2, :] = q_own[r, :, pl.ds(at, HEAD)].astype(F32)
        q_cls[c] = q_f32[c].astype(BF16)

    loop(0, 4, pack)

    def z_rows(at, n):
        return q_z.at[pl.ds(pl.multiple_of(16 * at, 16), 16 * n)]

    for d in (4, -4, 3, -3, 2, -2, 1, -1):
        remote(q_cls.at[rem(u + d + 4, 4)], z_rows(4 - d, 1), pair(s1), along(d, core)).start()
    q_z[64:80, :] = q_cls[u]

    def spread(what):
        def one(group, slot, to):
            src = features(v_ref if what else k_ref, group)
            dst = v_place(slot) if what else k_all.at[slot]
            remote(src, dst, (kv.at[2 * what], kv.at[2 * what + 1]), to).start()

        for d, slot in ((d2, 6 + core), (1, 2 + core), (-1, 4 + core)):
            for c in range(2):
                one(2 * rem(u + d + 4, 4) + c, slot, along(d, c))
        one(2 * u + 1 - core, 1, other)

    spread(0)

    blk = lax.broadcasted_iota(jnp.int32, (32, HEAD), 0)
    lane = lax.broadcasted_iota(jnp.int32, (32, HEAD), 1)
    half, step, side, sub = blk >> 4, (blk >> 2) & 3, (blk >> 1) & 1, 2 * (blk & 1) + (lane >> 6)
    ys = (y + jnp.where(side == 0, step, sub)) & 3
    xs = (x + jnp.where(side == 0, sub, step)) & 3
    cs = jnp.where((lane & 8) == 0, core, 1 - core)
    z_src = (z + 8 * half + 4 * side + ((lane >> 4) & 3) + 12) & 15
    which = 2 * (2 * xs + cs) + (z_src >> 3)
    block_at = jnp.zeros((32, HEAD), jnp.int32)
    for i in range(16):
        block_at = jnp.where(which == i, wb[i], block_at)
    within = (((z_src >> 2) & 1) * 4 + ys) * 8 + (z_src & 3) * 2 + (lane & 1)
    pos[...] = (64 * block_at + within).astype(F32)
    lane_f = lax.broadcasted_iota(jnp.int32, (1, HEAD), 1).astype(F32)
    sources = [(z, core), (z, 1 - core), (z - 1, 0), (z - 1, 1), (z + 1, 0), (z + 1, 1), (z - 2, 0), (z + 2, 1)]
    for j, (zt, c) in enumerate(sources):
        zt = rem(zt + 16, 16)
        base = div(zt, 4) * 16384 + y * 4096 + x * 1024 + c * 512 + rem(zt, 4) * 128
        key_pos[j:j + 1, :] = lane_f + base.astype(F32)

    def spread_pos(b):
        thr[b] = expand(pos[pl.ds(b, 1), :])

    def first_peer(a, i):
        return plane(0, i) if a else plane(i, 0)

    def second_peer(a, i):
        return plane(i, 0) if a else plane(0, i)

    def first(h):
        for a in range(2):
            mine = q_z.at[pl.ds(128 * h + 64 * a, 64)]

            def go(i):
                remote(mine, q_all.at[h, 0, a, 4 - i], (s3.at[h], s3r.at[h, a, 4 - i]), first_peer(a, i)).start()

            loop(1, 4, go)
        for a in range(2):
            mine = q_z.at[pl.ds(128 * h + 64 * a, 64)]

            def go_on(i):
                remote(mine, q_all.at[h, 4 - i, a, 0], (q4s.at[h], q4r.at[h, 4 - i]), second_peer(a, i)).start()

            loop(1, 4, go_on)
            q_all[h, 0, a, 0] = q_z[128 * h + 64 * a:128 * h + 64 * a + 64, :]

    def second(h):
        def pass_on(j):
            r = j + div(j, 2) - 2 * div(j, 3)
            for a in range(2):
                block = q_all.at[h, 0, a, r]
                arrived(block, (s3.at[h], s3r.at[h, a, r]))

                def go(i):
                    remote(block, q_all.at[h, 4 - i, a, r], (q4s.at[h], q4r.at[h, 4 - i]), second_peer(a, i)).start()

                loop(1, 4, go)

        loop(1, 4, pass_on)

    arrived(q_z.at[pl.ds(0, 128)], pair(s1))
    remote(z_rows(5, 4), z_rows(9, 4), pair(s2), along(-4, core)).start()
    remote(z_rows(1, 3), z_rows(13, 3), pair(s2), along(4, core)).start()
    first(0)

    spread(1)
    loop(0, 32, spread_pos)
    second(0)
    arrived(z_rows(9, 7), pair(s2))
    first(1)

    own_k.wait()
    own_v.wait()
    arrived(k_all.at[pl.ds(1, 7)], (kv.at[0], kv.at[1]))
    arrived(v_all.at[pl.ds(1, 7), :, pl.ds(0, HEAD)], (kv.at[2], kv.at[3]))

    eye = lax.broadcasted_iota(jnp.int32, (HEAD, HEAD), 0) == lax.broadcasted_iota(jnp.int32, (HEAD, HEAD), 1)

    def chunk(i):
        code = i - (div(i + 6, 8) - div(i + 3, 8)) + 3 * (div(i + 7, 8) - div(i + 6, 8))
        h, t = div(code, 4), rem(code, 4)

        @pl.when(i == 1)
        def _():
            second(1)

        @pl.when(t > 0)
        def _():
            arrived(q_all.at[h, t], (q4s.at[h], q4r.at[h, t]))

        for a in range(2):
            q = q_all[h, t, a].reshape(256, HEAD)
            scores = lax.dot_general(
                q, k_all[...].reshape(1024, HEAD), (((1,), (1,)), ((), ())), preferred_element_type=F32
            )
            limit = thr[pl.ds(4 * code + 2 * a, 2)].reshape(256, HEAD)
            parts = [
                jnp.where(key_pos[j:j + 1, :] <= limit, scores[:, j * HEAD:(j + 1) * HEAD], HIDDEN) for j in range(8)
            ]
            top = parts[0]
            for part in parts[1:]:
                top = jnp.maximum(top, part)
            top = jnp.max(top, axis=1, keepdims=True) * SCALE
            weights = jnp.concatenate([jnp.exp2(part * SCALE - top).astype(BF16) for part in parts], axis=1)
            both = lax.dot_general(
                weights, v_all[...].reshape(1024, 2 * HEAD), (((1,), (0,)), ((), ())), preferred_element_type=F32
            )
            total = both[:, HEAD:]
            o_all[h, t, a] = (both[:, :HEAD] / total).astype(BF16).reshape(2, HEAD, HEAD)
            level = top + jnp.log2(total)
            for r in range(2):
                l_all[h, t, a, r] = jnp.sum(
                    jnp.where(eye, level[r * HEAD:(r + 1) * HEAD], 0.0), axis=0, keepdims=True
                )

        @pl.when((t > 0) & (h == 0))
        def _():
            for a in range(2):
                to = second_peer(a, t)
                remote(o_all.at[0, t, a], o_in.at[4 - t, a], pair(os), to).start()
                remote(l_all.at[0, t, a], l_in.at[4 - t, a], pair(ls), to).start()

        @pl.when(h == 1)
        def _():
            for a in range(2):
                for sub in range(4):

                    @pl.when((t > 0) | (sub > 0))
                    def _():
                        back_t, back_sub = rem(4 - t, 4), (4 - sub) % 4
                        to = plane(t, sub) if a else plane(sub, t)
                        there = 4 * back_sub + back_t if a else 4 * back_t + back_sub
                        part = o_all.at[1, t, a, sub // 2, pl.ds(64 * (sub % 2), 64)]
                        remote(part, ob_in.at[there, pl.ds(64 * a, 64)], pair(obs), to).start()
                        remote(l_all.at[1, t, a, sub // 2], lb_in.at[there, a], pair(lbs), to).start()

    loop(0, 8, chunk)

    def z_part(ref, s):
        return ref.at[pl.ds(pl.multiple_of(16 * s, 16), 16)]

    def send_home(h, joined, level):
        z_out[128 * h:128 * h + 128, :] = joined.astype(BF16)
        lz_out[h] = level

        def go(i):
            s = 8 * h + rem(i + 4 * h, 8)

            @pl.when(s != 4)
            def _():
                to = along(s - 4, core)
                at = rem(20 - s, 16)
                remote(z_part(z_out, s), z_in.at[at], pair(zs), to).start()
                remote(lz_out.at[h], lz_in.at[at], pair(lzs), to).start()

        loop(0, 8, go)

    low = lax.broadcasted_iota(jnp.int32, (1, HEAD), 1) < 64

    def level_of(lower, lower_odd, upper, upper_odd):
        lower = pltpu.roll(lower, 64, 1) if lower_odd else lower
        upper = upper if upper_odd else pltpu.roll(upper, 64, 1)
        return jnp.where(low, lower, upper)

    def join_second():
        arrived(o_in.at[pl.ds(1, 3)], pair(os))
        arrived(l_in.at[pl.ds(1, 3)], pair(ls))

        def block(a, k):
            levels = [l_all[0, 0, a, k]] + [l_in[t, a, k] for t in range(1, 4)]
            level, shares = combine(levels)
            values = [o_all[0, 0, a, k]] + [o_in[t, a, k] for t in range(1, 4)]
            joined = weighted([expand(share) for share in shares], values).astype(BF16)
            lp_out[a, k] = level
            for m in range(2):
                sub = 2 * k + m
                p_out[sub, a] = joined[64 * m:64 * m + 64]

                @pl.when(sub > 0)
                def _():
                    to = first_peer(a, sub)
                    remote(p_out.at[sub, a], p_in.at[4 - sub, a], pair(ps), to).start()
                    remote(lp_out.at[a, k], lp_in.at[4 - sub, a], pair(lps), to).start()

        for a in range(2):
            loop(0, 2, lambda i, a=a: block(a, 1 - i))

    def join_first():
        arrived(p_in.at[pl.ds(1, 3)], pair(ps))
        arrived(lp_in.at[pl.ds(1, 3)], pair(lps))
        levels = [level_of(lp_out[0, 0], 0, lp_out[1, 0], 0)]
        levels += [level_of(lp_in[r, 0], r % 2, lp_in[r, 1], r % 2) for r in range(1, 4)]
        level, shares = combine(levels)
        values = [part.reshape(HEAD, HEAD) for part in [p_out[0]] + [p_in[r] for r in range(1, 4)]]
        send_home(0, weighted([expand(share) for share in shares], values), level)

    def join_plane():
        for a in range(2):
            ob_in[0, 64 * a:64 * a + 64, :] = o_all[1, 0, a, 0, 0:64, :]
            lb_in[0, a] = l_all[1, 0, a, 0]
        arrived(lb_in.at[pl.ds(1, 15)], pair(lbs))
        levels = [level_of(lb_in[n, 0], n % 2, lb_in[n, 1], (n // 4) % 2) for n in range(16)]
        top = levels[0]
        for level in levels[1:]:
            top = jnp.maximum(top, level)
        total = jnp.exp2(levels[0] - top)
        for level in levels[1:]:
            total = total + jnp.exp2(level - top)
        whole = top + jnp.log2(total)
        for n in range(16):
            share_b[n] = jnp.exp2(levels[n] - whole)
        arrived(ob_in.at[pl.ds(1, 15)], pair(obs))

        def add(i, acc):
            for m in range(4):
                acc = acc + expand(share_b[4 * i + m]) * ob_in[4 * i + m].astype(F32)
            return acc

        send_home(1, lax.fori_loop(0, 4, add, jnp.zeros((HEAD, HEAD), F32)), whole)

    join_second()
    join_first()
    join_plane()
    z_in[0] = z_out[64:80, :]
    lz_in[0] = lz_out[0]
    arrived(z_in.at[pl.ds(1, 15)], pair(zs))
    arrived(lz_in.at[pl.ds(1, 15)], pair(lzs))
    lane16 = lax.broadcasted_iota(jnp.int32, (16, HEAD), 1) - lax.broadcasted_iota(jnp.int32, (16, HEAD), 0)

    def join_z(w):
        levels, values = [], []
        for m in range(4):
            at = w + 4 * m
            offset = rem(20 - at, 8) * 16
            wide = jnp.broadcast_to(lz_in[at], (16, HEAD))
            levels.append(jnp.sum(jnp.where(lane16 == offset, wide, 0.0), axis=1, keepdims=True))
            values.append(z_in[at])
        _, shares = combine(levels)
        joined = weighted(shares, values)
        f_in[2 * rem(u + w, 4) + core] = joined[:8]
        s_out[w] = joined[8:]

    loop(0, 4, join_z)
    remote(s_out, s_in, pair(fs), other).start()
    arrived(s_in, pair(fs))

    def place(w):
        f_in[2 * rem(u + w, 4) + 1 - core] = s_in[w]

    loop(0, 4, place)

    def give(c):
        for g in range(4):
            at = pl.multiple_of((4 * c + g) * HEAD, HEAD)
            out_ref[:, pl.ds(at, HEAD)] = f_in[c, 2 * g:2 * g + 2, :].astype(BF16)

    loop(0, 8, give)

    sent(q_own.at[1], pair(swap))
    sent(q_z.at[pl.ds(0, 128)], pair(s1))
    sent(z_rows(9, 7), pair(s2))
    sent(k_all.at[pl.ds(1, 7)], (kv.at[0], kv.at[1]))
    sent(v_all.at[pl.ds(1, 7), :, pl.ds(0, HEAD)], (kv.at[2], kv.at[3]))
    for h in range(2):
        sent(q_all.at[h, 0, :, pl.ds(1, 3)], (s3.at[h], s3.at[h]))
        sent(q_all.at[h, pl.ds(1, 3)], (q4s.at[h], q4r.at[h, 0]))
    sent(o_in.at[pl.ds(1, 3)], pair(os))
    sent(l_in.at[pl.ds(1, 3)], pair(ls))
    sent(p_in.at[pl.ds(1, 3)], pair(ps))
    sent(lp_in.at[pl.ds(1, 3)], pair(lps))
    sent(ob_in.at[pl.ds(1, 15)], pair(obs))
    sent(lb_in.at[pl.ds(1, 15)], pair(lbs))
    sent(z_in.at[pl.ds(1, 15)], pair(zs))
    sent(lz_in.at[pl.ds(1, 15)], pair(lzs))
    sent(s_in, pair(fs))


def per_device(queries, keys, values, window_blocks):
    dma = pltpu.SemaphoreType.DMA
    vmem = pltpu.VMEM
    return pl.pallas_call(
        kernel,
        out_shape=jax.ShapeDtypeStruct(queries.shape, BF16),
        in_specs=[pl.BlockSpec(memory_space=pl.ANY)] * 4,
        out_specs=pl.BlockSpec(memory_space=pltpu.VMEM),
        scratch_shapes=[
            pltpu.SMEM((16,), jnp.int32),
            vmem((2, 2, 4096), BF16), vmem((4, 16, HEAD), F32), vmem((4, 16, HEAD), BF16), vmem((256, HEAD), BF16),
            vmem((2, 4, 2, 4, 64, HEAD), BF16), vmem((8, HEAD, HEAD), BF16), vmem((8, HEAD, 2 * HEAD), BF16),
            vmem((32, HEAD), F32), vmem((32, HEAD, HEAD), F32), vmem((8, HEAD), F32),
            vmem((2, 4, 2, 2, HEAD, HEAD), BF16), vmem((2, 4, 2, 2, 1, HEAD), F32),
            vmem((4, 2, 2, HEAD, HEAD), BF16), vmem((4, 2, 2, 1, HEAD), F32),
            vmem((4, 2, 64, HEAD), BF16), vmem((2, 2, 1, HEAD), F32),
            vmem((4, 2, 64, HEAD), BF16), vmem((4, 2, 1, HEAD), F32),
            vmem((16, HEAD, HEAD), BF16), vmem((16, 2, 1, HEAD), F32), vmem((16, 1, HEAD), F32),
            vmem((256, HEAD), BF16), vmem((2, 1, HEAD), F32),
            vmem((16, 16, HEAD), BF16), vmem((16, 1, HEAD), F32),
            vmem((4, 8, HEAD), F32), vmem((4, 8, HEAD), F32), vmem((8, 8, HEAD), F32),
            dma((4,)), dma((2,)), dma((2,)), dma((2,)), dma((2,)), dma((2, 2, 4)), dma((2,)), dma((2, 4)), dma((4,)),
            dma((2,)), dma((2,)), dma((2,)), dma((2,)), dma((2,)), dma((2,)), dma((2,)), dma((2,)), dma((2,)),
        ],
        compiler_params=pltpu.CompilerParams(
            collective_id=0, has_side_effects=True, vmem_limit_bytes=58 * 1024 * 1024
        ),
    )(queries, keys, values, window_blocks)


def solution(mesh):
    return jax.shard_map(
        per_device,
        mesh=mesh,
        in_specs=(
            P(("row", "col", "uly"), None),
            P(("col", "row", "uly"), None),
            P(("col", "row", "uly"), None),
            P(),
        ),
        out_specs=P(("row", "col", "uly"), None),
        check_vma=False,
    )
```

time: 59.8 us -> 57.6 us (0.963)
  Pallas kernels: 58.3 us -> 56 us
    pallas_call x1, Pallas kernels: 58.3 us -> 56 us  [per_device(): pl.pallas_call(kernel, out_shape=jax.ShapeDtypeStruct(queries.shape, BF16...]
where the time goes in v6:
time: 57.6 us; the launch traced here: 57.4 us
  Pallas kernels  56 us (97%)
  local copies, waits for them, and re-layouts  1.34 us (2%)
    pallas_call x1, Pallas kernels, per_device(): pl.pallas_call(kernel, out_shape=jax.ShapeDtypeStruct(queries.shape, BF16...  56 us
    unnamed x1, local copies, waits for them, and re-layouts  1.34 us

profile of v6, /device:TPU:1, one launch (start us, length us, event | category | flops | bytes accessed | tf_op | source)
XLA Modules:
  0.0 57.4 jit_solution(12958126131215853893)
XLA Ops:
  0.0 56.0 %shard_map.46 = bf16[2,4096]{1,0:T(2,128)(2,1)} custom-call(bf16[2,4096]{1,0:T(2,128)(2,1)} %q_ref.1, bf16[128,1024]{1,0:T(8,128)(2,1)} %k_ref.1, bf16[128,1024]{1,0:T(8,128)(2,1)} %v_ref.1, s32[16]{0:T(128)} %wb_ref.1), custom_call_target="tpu_custom_call" | custom-call | tf_op jit(solution)/shard_map/pallas_call | solution.py:428
  56.1 1.3 %copy.6 = bf16[2,4096]{1,0:T(2,128)(2,1)} copy(bf16[2,4096]{1,0:T(2,128)(2,1)} %shard_map.46) | data formatting | bytes 32768

commit v7 on v6

--- a/solution.py
+++ b/solution.py
@@ -9,7 +9,7 @@
 
 HEAD = 128
 MESH = pl.DeviceIdType.MESH
-SCALE = math.log2(math.e) / math.sqrt(HEAD)
+SCALE = 1.0 / math.sqrt(HEAD)
 HIDDEN = -1e30
 F32, BF16 = jnp.float32, jnp.bfloat16
 
@@ -20,10 +20,10 @@
 
 def combine(levels):
     top = jnp.maximum(jnp.maximum(levels[0], levels[1]), jnp.maximum(levels[2], levels[3]))
-    shares = [jnp.exp2(level - top) for level in levels]
+    shares = [jnp.exp(level - top) for level in levels]
     total = (shares[0] + shares[1]) + (shares[2] + shares[3])
     inverse = 1.0 / total
-    return top + jnp.log2(total), [share * inverse for share in shares]
+    return top + jnp.log(total), [share * inverse for share in shares]
 
 
 def weighted(shares, values):
@@ -84,13 +84,16 @@
     def greet(to):
         pl.semaphore_signal(barrier, inc=1, device_id=to, device_id_type=MESH)
 
-    for d in (4, -4, 3, -3, 2, -2, 1, -1):
+    for d in (4, -4, 3, -3, 2, -2):
         greet(along(d, core))
-    for i in (2, 1, 3):
-        greet(plane(i, 0))
-        greet(plane(0, i))
-    for d in (d2, 1, -1):
+    greet(plane(2, 0))
+    greet(plane(0, 2))
+    greet(along(d2, 1 - core))
+    for d in (1, -1):
         greet(along(d, 1 - core))
+        greet(along(d, core))
+        greet(plane(d + 4, 0))
+        greet(plane(0, d + 4))
     greet(other)
     own_q = pltpu.make_async_copy(q_ref, q_own.at[0], own.at[0])
     own_q.start()
@@ -248,13 +251,13 @@
             for part in parts[1:]:
                 top = jnp.maximum(top, part)
             top = jnp.max(top, axis=1, keepdims=True) * SCALE
-            weights = jnp.concatenate([jnp.exp2(part * SCALE - top).astype(BF16) for part in parts], axis=1)
+            weights = jnp.concatenate([jnp.exp(part * SCALE - top).astype(BF16) for part in parts], axis=1)
             both = lax.dot_general(
                 weights, v_all[...].reshape(1024, 2 * HEAD), (((1,), (0,)), ((), ())), preferred_element_type=F32
             )
             total = both[:, HEAD:]
             o_all[h, t, a] = (both[:, :HEAD] / total).astype(BF16).reshape(2, HEAD, HEAD)
-            level = top + jnp.log2(total)
+            level = top + jnp.log(total)
             for r in range(2):
                 l_all[h, t, a, r] = jnp.sum(
                     jnp.where(eye, level[r * HEAD:(r + 1) * HEAD], 0.0), axis=0, keepdims=True
@@ -350,12 +353,12 @@
         top = levels[0]
         for level in levels[1:]:
             top = jnp.maximum(top, level)
-        total = jnp.exp2(levels[0] - top)
+        total = jnp.exp(levels[0] - top)
         for level in levels[1:]:
-            total = total + jnp.exp2(level - top)
-        whole = top + jnp.log2(total)
+            total = total + jnp.exp(level - top)
+        whole = top + jnp.log(total)
         for n in range(16):
-            share_b[n] = jnp.exp2(levels[n] - whole)
+            share_b[n] = jnp.exp(levels[n] - whole)
         arrived(ob_in.at[pl.ds(1, 15)], pair(obs))
 
         def add(i, acc):
@@ -368,41 +371,6 @@
     join_second()
     join_first()
     join_plane()
-    z_in[0] = z_out[64:80, :]
-    lz_in[0] = lz_out[0]
-    arrived(z_in.at[pl.ds(1, 15)], pair(zs))
-    arrived(lz_in.at[pl.ds(1, 15)], pair(lzs))
-    lane16 = lax.broadcasted_iota(jnp.int32, (16, HEAD), 1) - lax.broadcasted_iota(jnp.int32, (16, HEAD), 0)
-
-    def join_z(w):
-        levels, values = [], []
-        for m in range(4):
-            at = w + 4 * m
-            offset = rem(20 - at, 8) * 16
-            wide = jnp.broadcast_to(lz_in[at], (16, HEAD))
-            levels.append(jnp.sum(jnp.where(lane16 == offset, wide, 0.0), axis=1, keepdims=True))
-            values.append(z_in[at])
-        _, shares = combine(levels)
-        joined = weighted(shares, values)
-        f_in[2 * rem(u + w, 4) + core] = joined[:8]
-        s_out[w] = joined[8:]
-
-    loop(0, 4, join_z)
-    remote(s_out, s_in, pair(fs), other).start()
-    arrived(s_in, pair(fs))
-
-    def place(w):
-        f_in[2 * rem(u + w, 4) + 1 - core] = s_in[w]
-
-    loop(0, 4, place)
-
-    def give(c):
-        for g in range(4):
-            at = pl.multiple_of((4 * c + g) * HEAD, HEAD)
-            out_ref[:, pl.ds(at, HEAD)] = f_in[c, 2 * g:2 * g + 2, :].astype(BF16)
-
-    loop(0, 8, give)
-
     sent(q_own.at[1], pair(swap))
     sent(q_z.at[pl.ds(0, 128)], pair(s1))
     sent(z_rows(9, 7), pair(s2))
@@ -417,6 +385,36 @@
     sent(lp_in.at[pl.ds(1, 3)], pair(lps))
     sent(ob_in.at[pl.ds(1, 15)], pair(obs))
     sent(lb_in.at[pl.ds(1, 15)], pair(lbs))
+    z_in[0] = z_out[64:80, :]
+    lz_in[0] = lz_out[0]
+    arrived(z_in.at[pl.ds(1, 15)], pair(zs))
+    arrived(lz_in.at[pl.ds(1, 15)], pair(lzs))
+    lane16 = lax.broadcasted_iota(jnp.int32, (16, HEAD), 1) - lax.broadcasted_iota(jnp.int32, (16, HEAD), 0)
+
+    def join_z(w):
+        levels, values = [], []
+        for m in range(4):
+            at = w + 4 * m
+            offset = rem(20 - at, 8) * 16
+            wide = jnp.broadcast_to(lz_in[at], (16, HEAD))
+            levels.append(jnp.sum(jnp.where(lane16 == offset, wide, 0.0), axis=1, keepdims=True))
+            values.append(z_in[at])
+        _, shares = combine(levels)
+        joined = weighted(shares, values)
+        f_in[w] = joined[:8]
+        s_out[w] = joined[8:]
+
+    loop(0, 4, join_z)
+    remote(s_out, s_in, pair(fs), other).start()
+
+    def give(w, c, heads):
+        for g in range(4):
+            at = pl.multiple_of((4 * (2 * rem(u + w, 4) + c) + g) * HEAD, HEAD)
+            out_ref[:, pl.ds(at, HEAD)] = heads[w, 2 * g:2 * g + 2, :].astype(BF16)
+
+    loop(0, 4, lambda w: give(w, core, f_in))
+    arrived(s_in, pair(fs))
+    loop(0, 4, lambda w: give(w, 1 - core, s_in))
     sent(z_in.at[pl.ds(1, 15)], pair(zs))
     sent(lz_in.at[pl.ds(1, 15)], pair(lzs))
     sent(s_in, pair(fs))
@@ -442,7 +440,7 @@
             vmem((16, HEAD, HEAD), BF16), vmem((16, 2, 1, HEAD), F32), vmem((16, 1, HEAD), F32),
             vmem((256, HEAD), BF16), vmem((2, 1, HEAD), F32),
             vmem((16, 16, HEAD), BF16), vmem((16, 1, HEAD), F32),
-            vmem((4, 8, HEAD), F32), vmem((4, 8, HEAD), F32), vmem((8, 8, HEAD), F32),
+            vmem((4, 8, HEAD), F32), vmem((4, 8, HEAD), F32), vmem((4, 8, HEAD), F32),
             dma((4,)), dma((2,)), dma((2,)), dma((2,)), dma((2,)), dma((2, 2, 4)), dma((2,)), dma((2, 4)), dma((4,)),
             dma((2,)), dma((2,)), dma((2,)), dma((2,)), dma((2,)), dma((2,)), dma((2,)), dma((2,)), dma((2,)),
         ],

time: 57.6 us -> 57.3 us (level)
  no operation moved by 1% of the time
where the time goes in v7:
time: 57.3 us; the launch traced here: 57.1 us
  Pallas kernels  55.8 us (97%)
  local copies, waits for them, and re-layouts  1.34 us (2%)
    pallas_call x1, Pallas kernels, per_device(): pl.pallas_call(kernel, out_shape=jax.ShapeDtypeStruct(queries.shape, BF16...  55.8 us
    unnamed x1, local copies, waits for them, and re-layouts  1.34 us

profile of v7, /device:TPU:1, one launch (start us, length us, event | category | flops | bytes accessed | tf_op | source)
XLA Modules:
  0.0 57.1 jit_solution(15856646814893704941)
XLA Ops:
  0.0 55.8 %shard_map.46 = bf16[2,4096]{1,0:T(2,128)(2,1)} custom-call(bf16[2,4096]{1,0:T(2,128)(2,1)} %q_ref.1, bf16[128,1024]{1,0:T(8,128)(2,1)} %k_ref.1, bf16[128,1024]{1,0:T(8,128)(2,1)} %v_ref.1, s32[16]{0:T(128)} %wb_ref.1), custom_call_target="tpu_custom_call" | custom-call | tf_op jit(solution)/shard_map/pallas_call | solution.py:426
  55.8 1.3 %copy.6 = bf16[2,4096]{1,0:T(2,128)(2,1)} copy(bf16[2,4096]{1,0:T(2,128)(2,1)} %shard_map.46) | data formatting | bytes 32768

commit v8 on v7

--- a/solution.py
+++ b/solution.py
@@ -104,14 +104,13 @@
         return ref.at[:, pl.ds(pl.multiple_of(group * HEAD, HEAD), HEAD)]
 
     def v_place(slot):
-        return v_all.at[slot, :, pl.ds(0, HEAD)]
+        return v_all.at[slot]
 
     my_group = 2 * u + core
     own_k = pltpu.make_async_copy(features(k_ref, my_group), k_all.at[0], own.at[2])
     own_v = pltpu.make_async_copy(features(v_ref, my_group), v_place(0), own.at[3])
     own_k.start()
     own_v.start()
-    v_all[:, :, HEAD:] = jnp.ones((8, HEAD, HEAD), BF16)
     pl.semaphore_wait(barrier, 18)
 
     remote(q_ref, q_own.at[1], pair(swap), other).start()
@@ -222,13 +221,14 @@
     own_k.wait()
     own_v.wait()
     arrived(k_all.at[pl.ds(1, 7)], (kv.at[0], kv.at[1]))
-    arrived(v_all.at[pl.ds(1, 7), :, pl.ds(0, HEAD)], (kv.at[2], kv.at[3]))
+    arrived(v_all.at[pl.ds(1, 7)], (kv.at[2], kv.at[3]))
 
     eye = lax.broadcasted_iota(jnp.int32, (HEAD, HEAD), 0) == lax.broadcasted_iota(jnp.int32, (HEAD, HEAD), 1)
 
     def chunk(i):
-        code = i - (div(i + 6, 8) - div(i + 3, 8)) + 3 * (div(i + 7, 8) - div(i + 6, 8))
-        h, t = div(code, 4), rem(code, 4)
+        h, t = div(i, 4), rem(i, 4)
+
+        pl.when(i == 7)(join_second)
 
         @pl.when(i == 1)
         def _():
@@ -243,7 +243,7 @@
             scores = lax.dot_general(
                 q, k_all[...].reshape(1024, HEAD), (((1,), (1,)), ((), ())), preferred_element_type=F32
             )
-            limit = thr[pl.ds(4 * code + 2 * a, 2)].reshape(256, HEAD)
+            limit = thr[pl.ds(4 * i + 2 * a, 2)].reshape(256, HEAD)
             parts = [
                 jnp.where(key_pos[j:j + 1, :] <= limit, scores[:, j * HEAD:(j + 1) * HEAD], HIDDEN) for j in range(8)
             ]
@@ -251,12 +251,15 @@
             for part in parts[1:]:
                 top = jnp.maximum(top, part)
             top = jnp.max(top, axis=1, keepdims=True) * SCALE
-            weights = jnp.concatenate([jnp.exp(part * SCALE - top).astype(BF16) for part in parts], axis=1)
-            both = lax.dot_general(
-                weights, v_all[...].reshape(1024, 2 * HEAD), (((1,), (0,)), ((), ())), preferred_element_type=F32
+            parts = [jnp.exp(part * SCALE - top) for part in parts]
+            total = (parts[0] + parts[1]) + (parts[2] + parts[3])
+            total = total + ((parts[4] + parts[5]) + (parts[6] + parts[7]))
+            total = jnp.sum(total, axis=1, keepdims=True)
+            weights = jnp.concatenate([part.astype(BF16) for part in parts], axis=1)
+            sums = lax.dot_general(
+                weights, v_all[...].reshape(1024, HEAD), (((1,), (0,)), ((), ())), preferred_element_type=F32
             )
-            total = both[:, HEAD:]
-            o_all[h, t, a] = (both[:, :HEAD] / total).astype(BF16).reshape(2, HEAD, HEAD)
+            o_all[h, t, a] = (sums / total).astype(BF16).reshape(2, HEAD, HEAD)
             level = top + jnp.log(total)
             for r in range(2):
                 l_all[h, t, a, r] = jnp.sum(
@@ -283,8 +286,6 @@
                         part = o_all.at[1, t, a, sub // 2, pl.ds(64 * (sub % 2), 64)]
                         remote(part, ob_in.at[there, pl.ds(64 * a, 64)], pair(obs), to).start()
                         remote(l_all.at[1, t, a, sub // 2], lb_in.at[there, a], pair(lbs), to).start()
-
-    loop(0, 8, chunk)
 
     def z_part(ref, s):
         return ref.at[pl.ds(pl.multiple_of(16 * s, 16), 16)]
@@ -368,14 +369,14 @@
 
         send_home(1, lax.fori_loop(0, 4, add, jnp.zeros((HEAD, HEAD), F32)), whole)
 
-    join_second()
+    loop(0, 8, chunk)
     join_first()
     join_plane()
     sent(q_own.at[1], pair(swap))
     sent(q_z.at[pl.ds(0, 128)], pair(s1))
     sent(z_rows(9, 7), pair(s2))
     sent(k_all.at[pl.ds(1, 7)], (kv.at[0], kv.at[1]))
-    sent(v_all.at[pl.ds(1, 7), :, pl.ds(0, HEAD)], (kv.at[2], kv.at[3]))
+    sent(v_all.at[pl.ds(1, 7)], (kv.at[2], kv.at[3]))
     for h in range(2):
         sent(q_all.at[h, 0, :, pl.ds(1, 3)], (s3.at[h], s3.at[h]))
         sent(q_all.at[h, pl.ds(1, 3)], (q4s.at[h], q4r.at[h, 0]))
@@ -431,7 +432,7 @@
         scratch_shapes=[
             pltpu.SMEM((16,), jnp.int32),
             vmem((2, 2, 4096), BF16), vmem((4, 16, HEAD), F32), vmem((4, 16, HEAD), BF16), vmem((256, HEAD), BF16),
-            vmem((2, 4, 2, 4, 64, HEAD), BF16), vmem((8, HEAD, HEAD), BF16), vmem((8, HEAD, 2 * HEAD), BF16),
+            vmem((2, 4, 2, 4, 64, HEAD), BF16), vmem((8, HEAD, HEAD), BF16), vmem((8, HEAD, HEAD), BF16),
             vmem((32, HEAD), F32), vmem((32, HEAD, HEAD), F32), vmem((8, HEAD), F32),
             vmem((2, 4, 2, 2, HEAD, HEAD), BF16), vmem((2, 4, 2, 2, 1, HEAD), F32),
             vmem((4, 2, 2, HEAD, HEAD), BF16), vmem((4, 2, 2, 1, HEAD), F32),

time: 57.3 us -> 56.9 us (level)
  no operation moved by 1% of the time
where the time goes in v8:
time: 56.9 us; the launch traced here: 56.7 us
  Pallas kernels  55.4 us (97%)
  local copies, waits for them, and re-layouts  1.34 us (2%)
    pallas_call x1, Pallas kernels, per_device(): pl.pallas_call(kernel, out_shape=jax.ShapeDtypeStruct(queries.shape, BF16...  55.4 us
    unnamed x1, local copies, waits for them, and re-layouts  1.34 us

profile of v8, /device:TPU:1, one launch (start us, length us, event | category | flops | bytes accessed | tf_op | source)
XLA Modules:
  0.0 56.7 jit_solution(2348799311496708982)
XLA Ops:
  0.0 55.4 %shard_map.46 = bf16[2,4096]{1,0:T(2,128)(2,1)} custom-call(bf16[2,4096]{1,0:T(2,128)(2,1)} %q_ref.1, bf16[128,1024]{1,0:T(8,128)(2,1)} %k_ref.1, bf16[128,1024]{1,0:T(8,128)(2,1)} %v_ref.1, s32[16]{0:T(128)} %wb_ref.1), custom_call_target="tpu_custom_call" | custom-call | tf_op jit(solution)/shard_map/pallas_call | solution.py:427
  55.4 1.3 %copy.6 = bf16[2,4096]{1,0:T(2,128)(2,1)} copy(bf16[2,4096]{1,0:T(2,128)(2,1)} %shard_map.46) | data formatting | bytes 32768
